TPU v7x, 32 devices: a whole 2x2x4 slice. The times are simulated.
32 devices in a mesh: row: 4 (over y, x), col: 8 (over z, core).
Axes of the slice: x: 2, y: 2, z: 4, core: 2. Of those that a mesh axis runs over, the one named last changes fastest.
Arguments:
- trailing: bfloat16 [4096, 8192], P('row', 'col'), may hold values from -6 to 6
- raw_l: bfloat16 [4, 16, 1024, 1024], P('row', None, 'col'), may hold values from -1.1953125 to 1.1953125
- raw_u: bfloat16 [16, 8, 1024, 1024], P(None, 'col', 'row'), may hold values from -1.1953125 to 1.1953125
- sketch: bfloat16 [4, 8, 1024, 192], P('row', 'col'), may hold values from -0.1875 to 0.1875
- helper_l: int32 [4, 16], P('row'), may hold values from 0 to 7, as said below
- helper_u: int32 [16, 8], P(None, 'col'), may hold values from 0 to 3, as said below
- ranks_l: int32 [4, 16], P('row'), may hold values from 64 to 192, as said below
- ranks_u: int32 [16, 8], P(None, 'col'), may hold values from 64 to 192, as said below
Outputs:
- updated: float32 [4096, 8192], P('row', 'col')
Inputs may be any that keep to these rules, and one draw needn't show every extreme that they name: `helper_l`: in every grid row no value occurs more than 4 times, and some value occurs exactly 4 times. `helper_u`: in every grid column no value occurs more than 8 times, and some value occurs exactly 8 times. `ranks_l`: some tile has rank 64 and some tile rank 192. `ranks_u`: some tile has rank 64 and some tile rank 192.
All inputs are finite; a program needn't handle non-finite values.
Results may differ from a plain program's by a relative error of at most 0.0068.
Values may be sent and summed in bfloat16 or wider, within the bound.
No kernel may reach another device: no remote copies, remote signals or barrier semaphores. Data moves between devices by JAX's collectives and lax.ppermute only.
A program may use at most 192 MiB of HBM per device.

v0:
```python
import functools

import jax
import jax.numpy as jnp
from jax import lax
from jax.experimental import pallas as pl
from jax.experimental.pallas import tpu as pltpu
from jax.sharding import PartitionSpec as P

NB = 32
PANEL = 8
HIGH = lax.Precision.HIGHEST
NN = (((1,), (0,)), ((), ()))
NT = (((1,), (1,)), ((), ()))
TN = (((0,), (0,)), ((), ()))


def mm(a, b, dims, precision=None):
    return lax.dot_general(a, b, dims, precision=precision, preferred_element_type=jnp.float32)


def invert_diagonal(blocks):
    nb = blocks[0].shape[0]
    row = lax.broadcasted_iota(jnp.int32, (nb, 2 * nb), 0)
    lane = lax.broadcasted_iota(jnp.int32, (nb, 2 * nb), 1)
    eye = (lane == row + nb).astype(jnp.float32)
    work = [jnp.concatenate([b, eye[:, nb:]], axis=1) for b in blocks]
    for p in range(0, nb, PANEL):
        spread = [
            [jnp.broadcast_to(a[:, j : j + 1], a.shape) for j in range(p, p + PANEL)] for a in work
        ]
        for i in range(min(PANEL, nb - 1 - p)):
            j = p + i
            for n, cols in enumerate(spread):
                factors = jnp.where(row > j, cols[i] * (1.0 / cols[i][j : j + 1, :]), 0.0)
                for k in range(i + 1, PANEL):
                    cols[k] = cols[k] - factors * cols[k][j : j + 1, :]
                work[n] = work[n] - factors * work[n][j : j + 1, :]
    out = []
    for a in work:
        d = jnp.sum(jnp.where(lane == row, a, 0.0), axis=1, keepdims=True)
        r = lax.rsqrt(d)
        r = r * (1.5 - 0.5 * d * r * r)
        out.append(a[:, nb:] * r)
    return out


def invert_cholesky(z_ref, n, width):
    for j in range(width // NB):
        lo, hi = j * NB, (j + 1) * NB
        inverses = invert_diagonal([z_ref[t, lo:hi, lo:hi] for t in range(n)])
        for t in range(n):
            panel = mm(inverses[t], z_ref[t, lo:hi, :], NN, HIGH)
            z_ref[t, lo:hi, :] = panel
            if hi < width:
                z_ref[t, hi:, :] = z_ref[t, hi:, :] - mm(panel[:, hi:width], panel, TN, HIGH)


SMEM = pl.BlockSpec(memory_space=pltpu.SMEM)
HBM = pl.BlockSpec(memory_space=pl.ANY)
VMEM = pl.BlockSpec(memory_space=pltpu.VMEM)


def factor_kernel(n_col, n_row, chunk, *refs):
    place, help_l, rank_l, help_u, rank_u = refs[:5]
    tile_l, raw_u, sk_col, own = refs[5:9]
    first_u = refs[9 : 8 + n_row]
    got_u = refs[8 + n_row : 7 + 2 * n_row]
    per = n_col // n_row
    made = refs[7 + 2 * n_row : 8 + 2 * n_row + per]
    omega, tile, sketched, z, sem, sem_s = refs[8 + 2 * n_row + per :]
    my_row, my_col = place[0], place[1]
    n, width, order = sketched.shape
    slab = order // n_row

    copies = []
    for t in range(n):
        if t == 0:
            k = chunk * n_col + my_col
            mine = [
                pltpu.make_async_copy(own, omega.at[t], sem_s.at[t]),
                pltpu.make_async_copy(tile_l, tile.at[t], sem.at[t, 0]),
            ]
            pltpu.make_async_copy(sk_col.at[help_l[k]], omega.at[t], sem_s.at[t]).start()
        else:
            k = chunk * n_col + (t - 1) * n_row + my_row
            mine = [pltpu.make_async_copy(own, omega.at[t], sem_s.at[t])]
            away = jnp.bitwise_xor(my_row, help_u[k])
            for o in range(n_row):

                @pl.when(away == o)
                def _(o=o, t=t):
                    src = first_u[o - 1].at[pl.ds(per * slab, width)] if o else own
                    pltpu.make_async_copy(src, omega.at[t], sem_s.at[t]).start()
            for d in range(n_row):
                j = jnp.bitwise_xor(my_row, d)
                src = raw_u.at[k] if d == 0 else got_u[d - 1].at[pl.ds((t - 1) * slab, slab)]
                dst = tile.at[t, pl.ds(pl.multiple_of(j * slab, slab), slab)]
                mine.append(pltpu.make_async_copy(src, dst, sem.at[t, d]))
        for c in mine[1:]:
            c.start()
        copies.append(mine)

    row = lax.broadcasted_iota(jnp.int32, (width, width), 0)
    lane = lax.broadcasted_iota(jnp.int32, (width, width), 1)
    eye = (row == lane).astype(jnp.float32)
    sub = lax.broadcasted_iota(jnp.int32, (width, order), 0)
    for t in range(n):
        for c in copies[t]:
            c.wait()
        if t == 0:
            q = rank_l[chunk * n_col + my_col]
        else:
            q = rank_u[chunk * n_col + (t - 1) * n_row + my_row]
        masked = jnp.where(sub < q, omega[t].astype(jnp.float32), 0.0).astype(jnp.bfloat16)
        sketched[t] = mm(masked, tile[t], NT)
        gram = mm(sketched[t], sketched[t], NT, HIGH) + jnp.where(row >= q, eye, 0.0)
        z[t] = jnp.concatenate([gram, eye], axis=1)
    invert_cholesky(z, n, width)
    for t in range(n):
        out = made[t]
        basis = mm(z[t, :, width:], sketched[t], NN, HIGH).astype(jnp.bfloat16)
        out[0] = basis
        out[1] = mm(basis, tile[t], NN).astype(jnp.bfloat16)


def factor(chunk, place, help_l, rank_l, help_u, rank_u, tile_l, raw_u, sk_col, own, first_u, got_u):
    n_col, n_row = sk_col.shape[0], len(got_u) + 1
    per = n_col // n_row
    n = 1 + per
    width, order = own.shape
    return pl.pallas_call(
        functools.partial(factor_kernel, n_col, n_row, chunk),
        out_shape=(jax.ShapeDtypeStruct((2, width, order), jnp.bfloat16),) * n,
        in_specs=[SMEM] * 5 + [HBM] * (2 + 2 * n_row),
        out_specs=(VMEM,) * n,
        scratch_shapes=[
            pltpu.VMEM((n, width, order), jnp.bfloat16),
            pltpu.VMEM((n, order, order), jnp.bfloat16),
            pltpu.VMEM((n, width, order), jnp.float32),
            pltpu.VMEM((n, width, 2 * width), jnp.float32),
            pltpu.SemaphoreType.DMA((n, n_row)),
            pltpu.SemaphoreType.DMA((n,)),
        ],
        compiler_params=pltpu.CompilerParams(vmem_limit_bytes=56 * 2**20),
        cost_estimate=pl.CostEstimate(flops=35 * 10**11, bytes_accessed=12 * 2**20, transcendentals=0),
        name="factor_tiles",
    )(place, help_l, rank_l, help_u, rank_u, tile_l, raw_u, sk_col, own, *first_u, *got_u)


def update_kernel(n_col, n_row, group, *refs):
    place, start, full_l = refs[:3]
    parts = refs[3 : 3 + n_col]
    out, ql, wl, qwu, left, acc, tr, sem, sem_l, sem_t, sem_o = refs[3 + n_col :]
    my_row = place[0]
    width = ql.shape[1]
    rounds = n_col // group
    block = 256
    blocks = start.shape[0] // block

    def load_l(g):
        at = pl.ds(g * group, group)
        return (
            pltpu.make_async_copy(full_l.at[at, 1], wl.at[at], sem_l.at[g, 1]),
            pltpu.make_async_copy(full_l.at[at, 0], ql.at[at], sem_l.at[g, 0]),
        )

    load = pltpu.make_async_copy(start, tr, sem_t)
    for g in range(rounds):
        for c in load_l(g):
            c.start()
        for i in range(g * group, (g + 1) * group):
            t, o = i // n_row, i % n_row
            k = t * n_row + jnp.bitwise_xor(my_row, o)
            pltpu.make_async_copy(parts[i], qwu.at[k], sem.at[k]).start()
    load.start()
    for g in range(rounds):
        for c in load_l(g):
            c.wait()
        for e in range(group):
            k = g * group + e
            pltpu.make_async_copy(parts[0], qwu.at[k], sem.at[k]).wait()
            mid = mm(qwu[k, 0], wl[k], NT).astype(jnp.bfloat16)
            left[e * width : (e + 1) * width, :] = mm(mid, ql[k], NN).astype(jnp.bfloat16)
        coeff = qwu[g * group : (g + 1) * group, 1].reshape(group * width, qwu.shape[3])
        if g == rounds - 1:
            load.wait()
        for b in range(blocks):
            at = slice(b * block, (b + 1) * block)
            part = mm(left[:, at], coeff, TN)
            if g:
                part = acc[at, :] + part
            if g == rounds - 1:
                acc[at, :] = tr[at, :].astype(jnp.float32) - part
                pltpu.make_async_copy(acc.at[at], out.at[at], sem_o.at[b]).start()
            else:
                acc[at, :] = part
    for b in range(blocks):
        at = slice(b * block, (b + 1) * block)
        pltpu.make_async_copy(acc.at[at], out.at[at], sem_o.at[b]).wait()


def update(place, start, full_l, parts):
    n_row = len(parts[0])
    n_col, _, width, order = full_l.shape
    group = 4
    held = pltpu.VMEM((n_col, width, order), jnp.bfloat16)
    return pl.pallas_call(
        functools.partial(update_kernel, n_col, n_row, group),
        out_shape=jax.ShapeDtypeStruct(start.shape, jnp.float32),
        in_specs=[SMEM] + [HBM] * (2 + n_col),
        out_specs=HBM,
        scratch_shapes=[
            held,
            held,
            pltpu.VMEM((n_col, 2, width, order), jnp.bfloat16),
            pltpu.VMEM((group * width, order), jnp.bfloat16),
            pltpu.VMEM(start.shape, jnp.float32),
            pltpu.VMEM(start.shape, start.dtype),
            pltpu.SemaphoreType.DMA((n_col,)),
            pltpu.SemaphoreType.DMA((n_col // group, 2)),
            pltpu.SemaphoreType.DMA,
            pltpu.SemaphoreType.DMA((start.shape[0] // 256,)),
        ],
        compiler_params=pltpu.CompilerParams(vmem_limit_bytes=56 * 2**20),
        cost_estimate=pl.CostEstimate(flops=15 * 10**11, bytes_accessed=20 * 2**20, transcendentals=0),
        name="update_tile",
    )(place, start, full_l, *(p for part in parts for p in part))


def shift(x, axis, size, move):
    return lax.ppermute(x, axis, [(i, move(i)) for i in range(size)])


def outgoing_u(raw, chunk, n_col, n_row):
    me = lax.axis_index("row")
    per = n_col // n_row
    x = raw.reshape((-1, per, n_row) + raw.shape[1:])
    return [
        lax.dynamic_slice(
            x, (chunk, 0, jnp.bitwise_xor(me, d), 0, 0), (1, per, 1) + raw.shape[1:]
        ).reshape(-1, raw.shape[2])
        for d in range(1, n_row)
    ]


def exchange_u(sent, n_row):
    return [shift(x, "row", n_row, lambda i: i ^ d) for d, x in enumerate(sent, 1)]


def gather_row(pieces, n_row):
    bits = [1 << b for b in range(n_row.bit_length() - 1)]
    out = []
    for number, piece in enumerate(pieces):
        turn = number % len(bits)
        held = {0: piece}
        for b in bits[turn:] + bits[:turn]:
            held.update({o ^ b: shift(p, "row", n_row, lambda i: i ^ b) for o, p in held.items()})
        out.append([held[o] for o in range(n_row)])
    return out


def local(trailing, raw_l, raw_u, sketch, helper_l, helper_u, ranks_l, ranks_u):
    n_col, n_row = lax.axis_size("col"), lax.axis_size("row")
    place = jnp.stack([lax.axis_index("row"), lax.axis_index("col")]).astype(jnp.int32)
    mine_l, mine_u = raw_l[0], raw_u[:, 0]
    chunks = mine_l.shape[0] // n_col
    own = jnp.swapaxes(sketch[0, 0], 0, 1)
    sk_col = lax.all_gather(own[None], "col", axis=0, tiled=True)
    result, full_l = trailing, None
    for c in range(chunks):
        tile_l = lax.all_to_all(mine_l[c * n_col : (c + 1) * n_col], "col", 0, 0, tiled=True)
        sent_u = outgoing_u(mine_u, c, n_col, n_row)
        if c == 0:
            sent_u = [jnp.concatenate([x, own]) for x in sent_u]
        got_u = exchange_u(sent_u, n_row)
        if c == 0:
            first_u = got_u
        made_l, *made_u = factor(
            c, place, helper_l[0], ranks_l[0], helper_u[:, 0], ranks_u[:, 0],
            tile_l.reshape(-1, tile_l.shape[2]), mine_u, sk_col, own, first_u, got_u,
        )
        if full_l is not None:
            full_l, made_l = lax.optimization_barrier((full_l, made_l))
            result = update(place, result, full_l, full_u)
        full_l = lax.all_gather(made_l[None], "col", axis=0, tiled=True)
        full_u = gather_row(made_u, n_row)
    return update(place, result, full_l, full_u)


def solution(mesh):
    placed = (
        P("row", "col"),
        P("row", None, "col", None),
        P(None, "col", "row", None),
        P("row", "col", None, None),
        P("row", None),
        P(None, "col"),
        P("row", None),
        P(None, "col"),
    )
    return jax.shard_map(
        local, mesh=mesh, in_specs=placed, out_specs=P("row", "col"), check_vma=False
    )
```

profile of v0, /device:TPU:0, one launch (start us, length us, event | category | flops | bytes accessed | tf_op | source)
XLA Modules:
  0.0 289.8 jit_solution(920198905109432243)
XLA Ops:
  7.3 4.9 %slice_bitcast_fusion = (bf16[8,128,1024]{2,1,0:T(8,128)(2,1)}, bf16[8,128,1024]{2,1,0:T(8,128)(2,1)}) fusion(bf16[1,16,128,1024]{3,2,1,0:T(8,128)(2,1)} %param.9), kind=kLoop, calls=%fused_computation.3 | loop fusion | bytes 8388608 | tf_op jit(solution)/shard_map/slice | solution.py:272
  12.2 6.3 %all-to-all-start = ((bf16[8,128,1024]{2,1,0:T(8,128)(2,1)}), bf16[8,128,1024]{2,1,0:T(8,128)(2,1)S(1)}, u32[]{:S(2)}, u32[]{:S(2)}) async-start(bf16[8,128,1024]{2,1,0:T(8,128)(2,1)} %get-tuple-element.28), calls=%async_computation | async-start | bytes 4194304 | tf_op jit(solution)/shard_map/all_to_all | solution.py:272
  18.5 5.2 %constant_dynamic-slice_fusion = (bf16[1,2,1,256,1024]{4,3,2,1,0:T(8,128)(2,1)}, bf16[1,2,1,256,1024]{4,3,2,1,0:T(8,128)(2,1)}, bf16[1,2,1,256,1024]{4,3,2,1,0:T...) fusion(bf16[2,2,4,256,1024]{4,3,2,1,0:T(8,128)(2,1)} %bitcast.3, ...), kind=kLoop, calls=%fused_computation.5 | loop fusion | bytes 12582924 | tf_op jit(solution)/shard_map/dynamic_slice | solution.py:240
  23.7 2.4 pad_maximum_fusion
  26.2 1.6 collective-permute-start
  29.6 1.6 collective-permute-start.3
  33.4 27.4 %collective-permute-done.refs_9_.refs_12_ = bf16[704,1024]{1,0:T(8,128)(2,1)S(1)} collective-permute-done((bf16[704,1024]{1,0:T(8,128)(2,1)}, bf16[704,1024]{1,0:T(8,128)(2,1)S(1)}, u32[]{:S(2)}, u32[]{:S(2)}) %collective-permute-start) | collective-permute-done | bytes 1441824 | tf_op jit(solution)/shard_map/ppermute | solution.py:232
  60.8 2.5 collective-permute-start.5
  63.3 29.6 %all-to-all-done = bf16[8,128,1024]{2,1,0:T(8,128)(2,1)S(1)} async-done(((bf16[8,128,1024]{2,1,0:T(8,128)(2,1)}), bf16[8,128,1024]{2,1,0:T(8,128)(2,1)S(1)}, u32[]{:S(2)}, u32[]{:S(2)}) %all-to-all-start) | async-done | bytes 2097184 | tf_op jit(solution)/shard_map/all_to_all | solution.py:272
  94.2 4.4 %all-to-all-start.1 = ((bf16[8,128,1024]{2,1,0:T(8,128)(2,1)}), bf16[8,128,1024]{2,1,0:T(8,128)(2,1)}, u32[]{:S(2)}, u32[]{:S(2)}) async-start(bf16[8,128,1024]{2,1,0:T(8,128)(2,1)} %get-tuple-element.27), calls=%async_computation.1 | async-start | bytes 4194304 | tf_op jit(solution)/shard_map/all_to_all | solution.py:272
  98.9 25.2 %factor_tiles.2 = (bf16[2,192,1024]{2,1,0:T(8,128)(2,1)}, bf16[2,192,1024]{2,1,0:T(8,128)(2,1)}, bf16[2,192,1024]{2,1,0:T(8,128)(2,1)}) custom-call(s32[2]{0:T(128)} %pad_add_fusion.refs_0_, s32[16]{0:T(128)} %bitcast.53, s32[16]{0:T(128)} %bitcast.55, s32[16]{0:T(128)} %bitcast.57, s32[16]{0:T(128)} %bitcast.59, bf16[1024,1024]{1,0:T(8,128)(2,1)} %bitcast.44, ...), custom_call_target="tpu_custom_call" | custom-call | flops 3499999887360 | bytes 12582912 | tf_op jit(solution)/shard_map/factor_tiles/pallas_call | solution.py:132
  124.1 1.6 collective-permute-start.6
  127.8 9.5 %collective-permute-done.4.refs_13_ = bf16[512,1024]{1,0:T(8,128)(2,1)} collective-permute-done((bf16[512,1024]{1,0:T(8,128)(2,1)}, bf16[512,1024]{1,0:T(8,128)(2,1)}, u32[]{:S(2)}, u32[]{:S(2)}) %collective-permute-start.4) | collective-permute-done | bytes 1048608 | tf_op jit(solution)/shard_map/ppermute | solution.py:232
  137.8 36.1 %all-to-all-done.1 = bf16[8,128,1024]{2,1,0:T(8,128)(2,1)} async-done(((bf16[8,128,1024]{2,1,0:T(8,128)(2,1)}), bf16[8,128,1024]{2,1,0:T(8,128)(2,1)}, u32[]{:S(2)}, u32[]{:S(2)}) %all-to-all-start.1) | async-done | bytes 2097184 | tf_op jit(solution)/shard_map/all_to_all | solution.py:272
  173.9 24.9 %factor_tiles.3 = (bf16[2,192,1024]{2,1,0:T(8,128)(2,1)}, bf16[2,192,1024]{2,1,0:T(8,128)(2,1)}, bf16[2,192,1024]{2,1,0:T(8,128)(2,1)}) custom-call(s32[2]{0:T(128)} %pad_add_fusion.refs_0_, s32[16]{0:T(128)} %bitcast.54, s32[16]{0:T(128)} %bitcast.56, s32[16]{0:T(128)} %bitcast.58, s32[16]{0:T(128)} %bitcast.60, bf16[1024,1024]{1,0:T(8,128)(2,1)} %bitcast.19.refs_5_, ...), custom_call_target="tpu_custom_call" | custom-call | flops 3499999887360 | bytes 12582912 | tf_op jit(solution)/shard_map/factor_tiles/pallas_call | solution.py:132
  198.8 1.6 collective-permute-start.12
  200.4 1.6 collective-permute-start.16
  203.0 1.6 collective-permute-start.13
  204.6 15.1 %collective-permute-done.12.refs_4_ = bf16[2,192,1024]{2,1,0:T(8,128)(2,1)} collective-permute-done((bf16[2,192,1024]{2,1,0:T(8,128)(2,1)}, bf16[2,192,1024]{2,1,0:T(8,128)(2,1)}, u32[]{:S(2)}, u32[]{:S(2)}) %collective-permute-start.12) | collective-permute-done | bytes 786464 | tf_op jit(solution)/shard_map/ppermute | solution.py:232
  222.7 13.7 %collective-permute-done.11.refs_10_ = bf16[2,192,1024]{2,1,0:T(8,128)(2,1)S(1)} collective-permute-done((bf16[2,192,1024]{2,1,0:T(8,128)(2,1)}, bf16[2,192,1024]{2,1,0:T(8,128)(2,1)S(1)}, u32[]{:S(2)}, u32[]{:S(2)}) %collective-permute-start.11) | collective-permute-done | bytes 786464 | tf_op jit(solution)/shard_map/ppermute | solution.py:232
  238.8 13.7 %update_tile.2.refs_1_ = f32[1024,1024]{1,0:T(8,128)} custom-call(s32[2]{0:T(128)} %pad_add_fusion.refs_0_, bf16[1024,1024]{1,0:T(8,128)(2,1)} %refs_1_.1, bf16[8,2,192,1024]{3,2,1,0:T(8,128)(2,1)} %bitcast.49, bf16[2,192,1024]{2,1,0:T(8,128)(2,1)} %get-tuple-element.16.refs_3_, bf16[2,192,1024]{2,1,0:T(8,128)(2,1)} %collective-permute-done.6.refs_4_, ...), custom_call_target="tpu_custom_call" | custom-call | flops 1500000026624 | bytes 20971520 | tf_op jit(solution)/shard_map/update_tile/pallas_call | solution.py:208
  252.6 2.3 collective-permute-done.13.refs_5_
  254.9 14.3 %collective-permute-done.14.refs_6_ = bf16[2,192,1024]{2,1,0:T(8,128)(2,1)} collective-permute-done((bf16[2,192,1024]{2,1,0:T(8,128)(2,1)}, bf16[2,192,1024]{2,1,0:T(8,128)(2,1)}, u32[]{:S(2)}, u32[]{:S(2)}) %collective-permute-start.14) | collective-permute-done | bytes 786464 | tf_op jit(solution)/shard_map/ppermute | solution.py:232
  269.2 13.9 %update_tile.3 = f32[1024,1024]{1,0:T(8,128)} custom-call(s32[2]{0:T(128)} %pad_add_fusion.refs_0_, f32[1024,1024]{1,0:T(8,128)} %update_tile.2.refs_1_, bf16[8,2,192,1024]{3,2,1,0:T(8,128)(2,1)} %bitcast.50, bf16[2,192,1024]{2,1,0:T(8,128)(2,1)} %get-tuple-element.19.refs_3_, bf16[2,192,1024]{2,1,0:T(8,128)(2,1)} %collective-permute-done.12.refs_4_, ...), custom_call_target="tpu_custom_call" | custom-call | flops 1500000026624 | bytes 20971520 | tf_op jit(solution)/shard_map/update_tile/pallas_call | solution.py:208
  (43 shorter events, 15.5 us)
Async XLA Ops:
  6.5 92.3 %all-gather.7.cloned.1.call-start = ((), (), s32[]{:S(2)}) async-start(), calls=%async_computation.2 | async-start | bytes 3538944 | tf_op jit(solution)/shard_map/all_gather | solution.py:269
  12.2 80.7 %all-to-all-start = ((bf16[8,128,1024]{2,1,0:T(8,128)(2,1)}), bf16[8,128,1024]{2,1,0:T(8,128)(2,1)S(1)}, u32[]{:S(2)}, u32[]{:S(2)}) async-start(bf16[8,128,1024]{2,1,0:T(8,128)(2,1)} %get-tuple-element.28), calls=%async_computation | async-start | bytes 4194304 | tf_op jit(solution)/shard_map/all_to_all | solution.py:272
  26.2 34.6 %collective-permute-start = (bf16[704,1024]{1,0:T(8,128)(2,1)}, bf16[704,1024]{1,0:T(8,128)(2,1)S(1)}, u32[]{:S(2)}, u32[]{:S(2)}) collective-permute-start(bf16[704,1024]{1,0:T(8,128)(2,1)} %get-tuple-element.31), channel_id=1, source_target_pairs={{0,8},{8,0},{16,24},{24,16},{1,9},{9,1},{17,25},{25,17},{2,10},{10... | collective-permute-start | bytes 4325384 | tf_op jit(solution)/shard_map/ppermute | solution.py:232
  27.7 71.1 %collective-permute-start.1 = (bf16[704,1024]{1,0:T(8,128)(2,1)}, bf16[704,1024]{1,0:T(8,128)(2,1)}, u32[]{:S(2)}, u32[]{:S(2)}) collective-permute-start(bf16[704,1024]{1,0:T(8,128)(2,1)} %get-tuple-element.30), channel_id=1, source_target_pairs={{0,16},{8,24},{16,0},{24,8},{1,17},{9,25},{17,1},{25,9},{2,18},{10... | collective-permute-start | bytes 4325384 | tf_op jit(solution)/shard_map/ppermute | solution.py:232
  29.2 69.6 %collective-permute-start.2 = (bf16[704,1024]{1,0:T(8,128)(2,1)}, bf16[704,1024]{1,0:T(8,128)(2,1)}, u32[]{:S(2)}, u32[]{:S(2)}) collective-permute-start(bf16[704,1024]{1,0:T(8,128)(2,1)} %get-tuple-element.29), channel_id=1, source_target_pairs={{0,24},{8,16},{16,8},{24,0},{1,25},{9,17},{17,9},{25,1},{2,26},{10... | collective-permute-start | bytes 4325384 | tf_op jit(solution)/shard_map/ppermute | solution.py:232
  29.6 97.6 %collective-permute-start.3 = (bf16[512,1024]{1,0:T(8,128)(2,1)}, bf16[512,1024]{1,0:T(8,128)(2,1)}, u32[]{:S(2)}, u32[]{:S(2)}) collective-permute-start(bf16[512,1024]{1,0:T(8,128)(2,1)} %bitcast.20), channel_id=1, source_target_pairs={{0,8},{8,0},{16,24},{24,16},{1,9},{9,1},{17,25},{25,17},{2,10},{10... | collective-permute-start | bytes 3145736 | tf_op jit(solution)/shard_map/ppermute | solution.py:232
  31.2 106.1 %collective-permute-start.4 = (bf16[512,1024]{1,0:T(8,128)(2,1)}, bf16[512,1024]{1,0:T(8,128)(2,1)}, u32[]{:S(2)}, u32[]{:S(2)}) collective-permute-start(bf16[512,1024]{1,0:T(8,128)(2,1)} %bitcast.21), channel_id=1, source_target_pairs={{0,16},{8,24},{16,0},{24,8},{1,17},{9,25},{17,1},{25,9},{2,18},{10... | collective-permute-start | bytes 3145736 | tf_op jit(solution)/shard_map/ppermute | solution.py:232
  60.8 32.1 %copy-start.2 = (bf16[704,1024]{1,0:T(8,128)(2,1)}, bf16[704,1024]{1,0:T(8,128)(2,1)S(1)}, u32[]{:S(2)}) copy-start(bf16[704,1024]{1,0:T(8,128)(2,1)S(1)} %collective-permute-done.refs_9_.refs_12_) | copy-start | bytes 4325380
  60.8 77.0 %collective-permute-start.5 = (bf16[512,1024]{1,0:T(8,128)(2,1)}, bf16[512,1024]{1,0:T(8,128)(2,1)}, u32[]{:S(2)}, u32[]{:S(2)}) collective-permute-start(bf16[512,1024]{1,0:T(8,128)(2,1)} %bitcast.22), channel_id=1, source_target_pairs={{0,24},{8,16},{16,8},{24,0},{1,25},{9,17},{17,9},{25,1},{2,26},{10... | collective-permute-start | bytes 3145736 | tf_op jit(solution)/shard_map/ppermute | solution.py:232
  94.2 79.7 %all-to-all-start.1 = ((bf16[8,128,1024]{2,1,0:T(8,128)(2,1)}), bf16[8,128,1024]{2,1,0:T(8,128)(2,1)}, u32[]{:S(2)}, u32[]{:S(2)}) async-start(bf16[8,128,1024]{2,1,0:T(8,128)(2,1)} %get-tuple-element.27), calls=%async_computation.1 | async-start | bytes 4194304 | tf_op jit(solution)/shard_map/all_to_all | solution.py:272
  98.6 104.3 %all-gather.9.cloned.1.call-start = ((), (), s32[]{:S(2)}) async-start(), calls=%async_computation.3 | async-start | bytes 7077888 | tf_op jit(solution)/shard_map/all_gather | solution.py:286
  124.1 77.9 %collective-permute-start.6 = (bf16[2,192,1024]{2,1,0:T(8,128)(2,1)}, bf16[2,192,1024]{2,1,0:T(8,128)(2,1)}, u32[]{:S(2)}, u32[]{:S(2)}) collective-permute-start(bf16[2,192,1024]{2,1,0:T(8,128)(2,1)} %get-tuple-element.16.refs_3_), channel_id=1, source_target_pairs={{0,8},{8,0},{16,24},{24,16},{1,9},{9,1},{17,25},{25,17},{2,10},{10... | collective-permute-start | bytes 2359304 | tf_op jit(solution)/shard_map/ppermute | solution.py:232
  125.6 76.9 %collective-permute-start.7 = (bf16[2,192,1024]{2,1,0:T(8,128)(2,1)}, bf16[2,192,1024]{2,1,0:T(8,128)(2,1)}, u32[]{:S(2)}, u32[]{:S(2)}) collective-permute-start(bf16[2,192,1024]{2,1,0:T(8,128)(2,1)} %get-tuple-element.16.refs_3_), channel_id=1, source_target_pairs={{0,16},{8,24},{16,0},{24,8},{1,17},{9,25},{17,1},{25,9},{2,18},{10... | collective-permute-start | bytes 2359304 | tf_op jit(solution)/shard_map/ppermute | solution.py:232
  127.2 142.0 %all-gather.11.cloned.1.call-start = ((), (), s32[]{:S(2)}) async-start(), calls=%async_computation.4 | async-start | bytes 7077888 | tf_op jit(solution)/shard_map/all_gather | solution.py:286
  127.2 73.2 %collective-permute-start.10 = (bf16[2,192,1024]{2,1,0:T(8,128)(2,1)}, bf16[2,192,1024]{2,1,0:T(8,128)(2,1)}, u32[]{:S(2)}, u32[]{:S(2)}) collective-permute-start(bf16[2,192,1024]{2,1,0:T(8,128)(2,1)} %get-tuple-element.17.refs_7_), channel_id=1, source_target_pairs={{0,16},{8,24},{16,0},{24,8},{1,17},{9,25},{17,1},{25,9},{2,18},{10... | collective-permute-start | bytes 2359304 | tf_op jit(solution)/shard_map/ppermute | solution.py:232
  137.3 65.7 %collective-permute-start.9 = (bf16[2,192,1024]{2,1,0:T(8,128)(2,1)}, bf16[2,192,1024]{2,1,0:T(8,128)(2,1)}, u32[]{:S(2)}, u32[]{:S(2)}) collective-permute-start(bf16[2,192,1024]{2,1,0:T(8,128)(2,1)} %get-tuple-element.17.refs_7_), channel_id=1, source_target_pairs={{0,8},{8,0},{16,24},{24,16},{1,9},{9,1},{17,25},{25,17},{2,10},{10... | collective-permute-start | bytes 2359304 | tf_op jit(solution)/shard_map/ppermute | solution.py:232
  198.8 20.9 %collective-permute-start.12 = (bf16[2,192,1024]{2,1,0:T(8,128)(2,1)}, bf16[2,192,1024]{2,1,0:T(8,128)(2,1)}, u32[]{:S(2)}, u32[]{:S(2)}) collective-permute-start(bf16[2,192,1024]{2,1,0:T(8,128)(2,1)} %get-tuple-element.19.refs_3_), channel_id=1, source_target_pairs={{0,8},{8,0},{16,24},{24,16},{1,9},{9,1},{17,25},{25,17},{2,10},{10... | collective-permute-start | bytes 2359304 | tf_op jit(solution)/shard_map/ppermute | solution.py:232
  200.4 20.8 %collective-permute-start.16 = (bf16[2,192,1024]{2,1,0:T(8,128)(2,1)}, bf16[2,192,1024]{2,1,0:T(8,128)(2,1)}, u32[]{:S(2)}, u32[]{:S(2)}) collective-permute-start(bf16[2,192,1024]{2,1,0:T(8,128)(2,1)} %get-tuple-element.20.refs_7_), channel_id=1, source_target_pairs={{0,16},{8,24},{16,0},{24,8},{1,17},{9,25},{17,1},{25,9},{2,18},{10... | collective-permute-start | bytes 2359304 | tf_op jit(solution)/shard_map/ppermute | solution.py:232
  202.0 34.5 %collective-permute-start.11 = (bf16[2,192,1024]{2,1,0:T(8,128)(2,1)}, bf16[2,192,1024]{2,1,0:T(8,128)(2,1)S(1)}, u32[]{:S(2)}, u32[]{:S(2)}) collective-permute-start(bf16[2,192,1024]{2,1,0:T(8,128)(2,1)} %collective-permute-done.10.refs_9_), channel_id=1, source_target_pairs={{0,8},{8,0},{16,24},{24,16},{1,9},{9,1},{17,25},{25,17},{2,10},{10... | collective-permute-start | bytes 2359304 | tf_op jit(solution)/shard_map/ppermute | solution.py:232
  202.5 35.5 %collective-permute-start.8 = (bf16[2,192,1024]{2,1,0:T(8,128)(2,1)}, bf16[2,192,1024]{2,1,0:T(8,128)(2,1)S(1)}, u32[]{:S(2)}, u32[]{:S(2)}) collective-permute-start(bf16[2,192,1024]{2,1,0:T(8,128)(2,1)} %collective-permute-done.6.refs_4_), channel_id=1, source_target_pairs={{0,16},{8,24},{16,0},{24,8},{1,17},{9,25},{17,1},{25,9},{2,18},{10... | collective-permute-start | bytes 2359304 | tf_op jit(solution)/shard_map/ppermute | solution.py:232
  203.0 51.9 %collective-permute-start.13 = (bf16[2,192,1024]{2,1,0:T(8,128)(2,1)}, bf16[2,192,1024]{2,1,0:T(8,128)(2,1)}, u32[]{:S(2)}, u32[]{:S(2)}) collective-permute-start(bf16[2,192,1024]{2,1,0:T(8,128)(2,1)} %get-tuple-element.19.refs_3_), channel_id=1, source_target_pairs={{0,16},{8,24},{16,0},{24,8},{1,17},{9,25},{17,1},{25,9},{2,18},{10... | collective-permute-start | bytes 2359304 | tf_op jit(solution)/shard_map/ppermute | solution.py:232
  219.7 35.2 %collective-permute-start.15 = (bf16[2,192,1024]{2,1,0:T(8,128)(2,1)}, bf16[2,192,1024]{2,1,0:T(8,128)(2,1)}, u32[]{:S(2)}, u32[]{:S(2)}) collective-permute-start(bf16[2,192,1024]{2,1,0:T(8,128)(2,1)} %get-tuple-element.20.refs_7_), channel_id=1, source_target_pairs={{0,8},{8,0},{16,24},{24,16},{1,9},{9,1},{17,25},{25,17},{2,10},{10... | collective-permute-start | bytes 2359304 | tf_op jit(solution)/shard_map/ppermute | solution.py:232
  221.2 48.0 %collective-permute-start.14 = (bf16[2,192,1024]{2,1,0:T(8,128)(2,1)}, bf16[2,192,1024]{2,1,0:T(8,128)(2,1)}, u32[]{:S(2)}, u32[]{:S(2)}) collective-permute-start(bf16[2,192,1024]{2,1,0:T(8,128)(2,1)} %collective-permute-done.12.refs_4_), channel_id=1, source_target_pairs={{0,16},{8,24},{16,0},{24,8},{1,17},{9,25},{17,1},{25,9},{2,18},{10... | collective-permute-start | bytes 2359304 | tf_op jit(solution)/shard_map/ppermute | solution.py:232
  236.4 32.8 %collective-permute-start.17 = (bf16[2,192,1024]{2,1,0:T(8,128)(2,1)}, bf16[2,192,1024]{2,1,0:T(8,128)(2,1)}, u32[]{:S(2)}, u32[]{:S(2)}) collective-permute-start(bf16[2,192,1024]{2,1,0:T(8,128)(2,1)} %collective-permute-done.16.refs_9_), channel_id=1, source_target_pairs={{0,8},{8,0},{16,24},{24,16},{1,9},{9,1},{17,25},{25,17},{2,10},{10... | collective-permute-start | bytes 2359304 | tf_op jit(solution)/shard_map/ppermute | solution.py:232
  (4 other events, 9.0 us)
Sparse Core Ops, SparseCore 0:
  9.0 75.9 all-gather.6
  127.3 72.7 all-gather.8
  203.1 63.4 all-gather.10
where the time goes:
time: 293 us; the launch traced here: 290 us
  waiting for transfers between devices  149 us (51%)
  Pallas kernels  77.7 us (27%)
  starting transfers between devices  34 us (12%)
  between operations  13.4 us (5%)
  local copies, waits for them, and re-layouts  12.4 us (4%)
  other arithmetic  3.08 us (1%)
    ppermute x18, waiting for transfers between devices, shift(): return lax.ppermute(x, axis, [(i, move(i)) for i in range(size)])  82.8 us
    all_to_all x2, waiting for transfers between devices, local(): lax.all_to_all(mine_l[c * n_col:(c + 1) * n_col], 'col', 0, 0, tiled=True)  65.7 us
    pallas_call x2, Pallas kernels, factor(): pl.pallas_call(functools.partial(factor_kernel, n_col, n_row, chunk), out...  50.1 us
    pallas_call x2, Pallas kernels, update(): pl.pallas_call(functools.partial(update_kernel, n_col, n_row, group), out...  27.6 us
    ppermute x18, starting transfers between devices, shift(): return lax.ppermute(x, axis, [(i, move(i)) for i in range(size)])  23 us
    all_to_all x2, starting transfers between devices, local(): lax.all_to_all(mine_l[c * n_col:(c + 1) * n_col], 'col', 0, 0, tiled=True)  10.7 us
  transfers between devices with their start and end apart: 23, of which 9 were waited for; matrix products, arithmetic and copies ran while one was open for 5% of the time, Pallas kernels for 22%

commit v1 on v0

--- a/solution.py
+++ b/solution.py
@@ -9,6 +9,7 @@
 
 NB = 32
 PANEL = 8
+VMEM_UPDATE = 50
 HIGH = lax.Precision.HIGHEST
 NN = (((1,), (0,)), ((), ()))
 NT = (((1,), (1,)), ((), ()))
@@ -61,14 +62,15 @@
 VMEM = pl.BlockSpec(memory_space=pltpu.VMEM)
 
 
-def factor_kernel(n_col, n_row, chunk, *refs):
+def factor_kernel(n_col, n_row, chunk, joined, *refs):
     place, help_l, rank_l, help_u, rank_u = refs[:5]
     tile_l, raw_u, sk_col, own = refs[5:9]
     first_u = refs[9 : 8 + n_row]
     got_u = refs[8 + n_row : 7 + 2 * n_row]
     per = n_col // n_row
-    made = refs[7 + 2 * n_row : 8 + 2 * n_row + per]
-    omega, tile, sketched, z, sem, sem_s = refs[8 + 2 * n_row + per :]
+    outs = 2 if joined else 1 + per
+    made = refs[7 + 2 * n_row : 7 + 2 * n_row + outs]
+    omega, tile, sketched, z, sem, sem_s = refs[7 + 2 * n_row + outs :]
     my_row, my_col = place[0], place[1]
     n, width, order = sketched.shape
     slab = order // n_row
@@ -118,22 +120,25 @@
         z[t] = jnp.concatenate([gram, eye], axis=1)
     invert_cholesky(z, n, width)
     for t in range(n):
-        out = made[t]
+        out = made[1].at[t - 1] if joined and t else made[t]
         basis = mm(z[t, :, width:], sketched[t], NN, HIGH).astype(jnp.bfloat16)
         out[0] = basis
         out[1] = mm(basis, tile[t], NN).astype(jnp.bfloat16)
 
 
-def factor(chunk, place, help_l, rank_l, help_u, rank_u, tile_l, raw_u, sk_col, own, first_u, got_u):
+def factor(chunk, place, help_l, rank_l, help_u, rank_u, tile_l, raw_u, sk_col, own, first_u, got_u, joined):
     n_col, n_row = sk_col.shape[0], len(got_u) + 1
     per = n_col // n_row
     n = 1 + per
     width, order = own.shape
+    one = jax.ShapeDtypeStruct((2, width, order), jnp.bfloat16)
+    both = jax.ShapeDtypeStruct((per, 2, width, order), jnp.bfloat16)
+    made = (one, both) if joined else (one,) * n
     return pl.pallas_call(
-        functools.partial(factor_kernel, n_col, n_row, chunk),
-        out_shape=(jax.ShapeDtypeStruct((2, width, order), jnp.bfloat16),) * n,
+        functools.partial(factor_kernel, n_col, n_row, chunk, joined),
+        out_shape=made,
         in_specs=[SMEM] * 5 + [HBM] * (2 + 2 * n_row),
-        out_specs=(VMEM,) * n,
+        out_specs=(VMEM,) * len(made),
         scratch_shapes=[
             pltpu.VMEM((n, width, order), jnp.bfloat16),
             pltpu.VMEM((n, order, order), jnp.bfloat16),
@@ -148,84 +153,77 @@
     )(place, help_l, rank_l, help_u, rank_u, tile_l, raw_u, sk_col, own, *first_u, *got_u)
 
 
-def update_kernel(n_col, n_row, group, *refs):
+def update_kernel(n_col, n_row, *refs):
     place, start, full_l = refs[:3]
-    parts = refs[3 : 3 + n_col]
-    out, ql, wl, qwu, left, acc, tr, sem, sem_l, sem_t, sem_o = refs[3 + n_col :]
+    out, ql, wl, left, acc, sem_l, sem_o = refs[-7:]
+    parts = refs[3:-7]
+    if len(parts) == n_row:
+        parts = [p.at[t] for t in range(n_col // n_row) for p in parts]
     my_row = place[0]
     width = ql.shape[1]
-    rounds = n_col // group
+    rounds = n_col // n_row
     block = 256
     blocks = start.shape[0] // block
 
     def load_l(g):
-        at = pl.ds(g * group, group)
+        at = pl.ds(g * n_row, n_row)
         return (
             pltpu.make_async_copy(full_l.at[at, 1], wl.at[at], sem_l.at[g, 1]),
             pltpu.make_async_copy(full_l.at[at, 0], ql.at[at], sem_l.at[g, 0]),
         )
 
-    load = pltpu.make_async_copy(start, tr, sem_t)
     for g in range(rounds):
         for c in load_l(g):
             c.start()
-        for i in range(g * group, (g + 1) * group):
-            t, o = i // n_row, i % n_row
-            k = t * n_row + jnp.bitwise_xor(my_row, o)
-            pltpu.make_async_copy(parts[i], qwu.at[k], sem.at[k]).start()
-    load.start()
     for g in range(rounds):
-        for c in load_l(g):
-            c.wait()
-        for e in range(group):
-            k = g * group + e
-            pltpu.make_async_copy(parts[0], qwu.at[k], sem.at[k]).wait()
-            mid = mm(qwu[k, 0], wl[k], NT).astype(jnp.bfloat16)
-            left[e * width : (e + 1) * width, :] = mm(mid, ql[k], NN).astype(jnp.bfloat16)
-        coeff = qwu[g * group : (g + 1) * group, 1].reshape(group * width, qwu.shape[3])
-        if g == rounds - 1:
-            load.wait()
+        mine = parts[g * n_row : (g + 1) * n_row]
+        load_w, load_q = load_l(g)
+        load_w.wait()
+        mids = []
+        for o, part in enumerate(mine):
+            k = g * n_row + jnp.bitwise_xor(my_row, o)
+            mids.append(mm(part[0], wl[k], NT).astype(jnp.bfloat16))
+        load_q.wait()
+        for o, mid in enumerate(mids):
+            k = g * n_row + jnp.bitwise_xor(my_row, o)
+            left[o * width : (o + 1) * width, :] = mm(mid, ql[k], NN).astype(jnp.bfloat16)
+        coeff = jnp.concatenate([part[1] for part in mine], axis=0)
         for b in range(blocks):
             at = slice(b * block, (b + 1) * block)
-            part = mm(left[:, at], coeff, TN)
+            done = mm(left[:, at], coeff, TN)
             if g:
-                part = acc[at, :] + part
+                done = acc[at, :] + done
             if g == rounds - 1:
-                acc[at, :] = tr[at, :].astype(jnp.float32) - part
+                acc[at, :] = start[at, :].astype(jnp.float32) - done
                 pltpu.make_async_copy(acc.at[at], out.at[at], sem_o.at[b]).start()
             else:
-                acc[at, :] = part
+                acc[at, :] = done
     for b in range(blocks):
         at = slice(b * block, (b + 1) * block)
         pltpu.make_async_copy(acc.at[at], out.at[at], sem_o.at[b]).wait()
 
 
 def update(place, start, full_l, parts):
-    n_row = len(parts[0])
+    n_row = lax.axis_size("row")
     n_col, _, width, order = full_l.shape
-    group = 4
     held = pltpu.VMEM((n_col, width, order), jnp.bfloat16)
     return pl.pallas_call(
-        functools.partial(update_kernel, n_col, n_row, group),
+        functools.partial(update_kernel, n_col, n_row),
         out_shape=jax.ShapeDtypeStruct(start.shape, jnp.float32),
-        in_specs=[SMEM] + [HBM] * (2 + n_col),
+        in_specs=[SMEM, VMEM, HBM] + [VMEM] * len(parts),
         out_specs=HBM,
         scratch_shapes=[
             held,
             held,
-            pltpu.VMEM((n_col, 2, width, order), jnp.bfloat16),
-            pltpu.VMEM((group * width, order), jnp.bfloat16),
+            pltpu.VMEM((n_row * width, order), jnp.bfloat16),
             pltpu.VMEM(start.shape, jnp.float32),
-            pltpu.VMEM(start.shape, start.dtype),
-            pltpu.SemaphoreType.DMA((n_col,)),
-            pltpu.SemaphoreType.DMA((n_col // group, 2)),
-            pltpu.SemaphoreType.DMA,
+            pltpu.SemaphoreType.DMA((n_col // n_row, 2)),
             pltpu.SemaphoreType.DMA((start.shape[0] // 256,)),
         ],
-        compiler_params=pltpu.CompilerParams(vmem_limit_bytes=56 * 2**20),
+        compiler_params=pltpu.CompilerParams(vmem_limit_bytes=VMEM_UPDATE * 2**20),
         cost_estimate=pl.CostEstimate(flops=15 * 10**11, bytes_accessed=20 * 2**20, transcendentals=0),
         name="update_tile",
-    )(place, start, full_l, *(p for part in parts for p in part))
+    )(place, start, full_l, *parts)
 
 
 def shift(x, axis, size, move):
@@ -248,6 +246,10 @@
     return [shift(x, "row", n_row, lambda i: i ^ d) for d, x in enumerate(sent, 1)]
 
 
+def spread_row(x, n_row):
+    return [x] + [shift(x, "row", n_row, lambda i: i ^ o) for o in range(1, n_row)]
+
+
 def gather_row(pieces, n_row):
     bits = [1 << b for b in range(n_row.bit_length() - 1)]
     out = []
@@ -256,7 +258,7 @@
         held = {0: piece}
         for b in bits[turn:] + bits[:turn]:
             held.update({o ^ b: shift(p, "row", n_row, lambda i: i ^ b) for o, p in held.items()})
-        out.append([held[o] for o in range(n_row)])
+        out += [held[o] for o in range(n_row)]
     return out
 
 
@@ -269,6 +271,8 @@
     sk_col = lax.all_gather(own[None], "col", axis=0, tiled=True)
     result, full_l = trailing, None
     for c in range(chunks):
+        if c == 1:
+            mine_l, first_u[0] = lax.optimization_barrier((mine_l, first_u[0]))
         tile_l = lax.all_to_all(mine_l[c * n_col : (c + 1) * n_col], "col", 0, 0, tiled=True)
         sent_u = outgoing_u(mine_u, c, n_col, n_row)
         if c == 0:
@@ -279,12 +283,14 @@
         made_l, *made_u = factor(
             c, place, helper_l[0], ranks_l[0], helper_u[:, 0], ranks_u[:, 0],
             tile_l.reshape(-1, tile_l.shape[2]), mine_u, sk_col, own, first_u, got_u,
+            c + 1 < chunks,
         )
         if full_l is not None:
             full_l, made_l = lax.optimization_barrier((full_l, made_l))
             result = update(place, result, full_l, full_u)
         full_l = lax.all_gather(made_l[None], "col", axis=0, tiled=True)
-        full_u = gather_row(made_u, n_row)
+        last = c + 1 == chunks
+        full_u = gather_row(made_u, n_row) if last else spread_row(made_u[0], n_row)
     return update(place, result, full_l, full_u)
 
 

time: 293 us -> 285 us (0.973)
  Pallas kernels: 77.7 us -> 73.3 us
    all_gather x2, waiting for transfers between devices: 0.01 us -> 7.03 us  [local(): full_l = lax.all_gather(made_l[None], 'col', axis=0, tiled=True)]
    ppermute x18 -> x15, waiting for transfers between devices: 82.8 us -> 77.7 us  [shift(): return lax.ppermute(x, axis, [(i, move(i)) for i in range(size)])]
    pallas_call x4, Pallas kernels: 77.7 us -> 73.3 us  [the longest x2 50.5 us: factor(): pl.pallas_call(functools.partial(factor_kernel, n_col, n_row, chunk, join...]
    all_to_all x2, waiting for transfers between devices: 65.7 us -> 62.7 us  [local(): lax.all_to_all(mine_l[c * n_col:(c + 1) * n_col], 'col', 0, 0, tiled=True)]
    ppermute x18 -> x15, starting transfers between devices: 23 us -> 20.2 us  [shift(): return lax.ppermute(x, axis, [(i, move(i)) for i in range(size)])]
    slice x1 -> x2, local copies, waits for them, and re-layouts: 4.92 us -> 6.25 us  [local(): mine_l[c * n_col:(c + 1) * n_col]]
  transfers between devices with their start and end apart: 23 -> 20, of which waited for: 9 -> 11; matrix products, arithmetic and copies ran while one was open for 5% -> 5% of each run, Pallas kernels for 22% -> 22%
where the time goes in v1:
time: 285 us; the launch traced here: 282 us
  waiting for transfers between devices  148 us (52%)
  Pallas kernels  73.3 us (26%)
  starting transfers between devices  31.1 us (11%)
  between operations  13.4 us (5%)
  local copies, waits for them, and re-layouts  12.7 us (4%)
  other arithmetic  2.96 us (1%)
    ppermute x15, waiting for transfers between devices, shift(): return lax.ppermute(x, axis, [(i, move(i)) for i in range(size)])  77.7 us
    all_to_all x2, waiting for transfers between devices, local(): lax.all_to_all(mine_l[c * n_col:(c + 1) * n_col], 'col', 0, 0, tiled=True)  62.7 us
    pallas_call x2, Pallas kernels, factor(): pl.pallas_call(functools.partial(factor_kernel, n_col, n_row, chunk, join...  50.5 us
    pallas_call x2, Pallas kernels, update(): pl.pallas_call(functools.partial(update_kernel, n_col, n_row), out_shape=...  22.8 us
    ppermute x15, starting transfers between devices, shift(): return lax.ppermute(x, axis, [(i, move(i)) for i in range(size)])  20.2 us
    all_to_all x2, starting transfers between devices, local(): lax.all_to_all(mine_l[c * n_col:(c + 1) * n_col], 'col', 0, 0, tiled=True)  10.7 us
    all_gather x2, waiting for transfers between devices, local(): full_l = lax.all_gather(made_l[None], 'col', axis=0, tiled=True)  7.03 us
    slice x2, local copies, waits for them, and re-layouts, local(): mine_l[c * n_col:(c + 1) * n_col]  6.25 us
  transfers between devices with their start and end apart: 20, of which 11 were waited for; matrix products, arithmetic and copies ran while one was open for 5% of the time, Pallas kernels for 22%

profile of v1, /device:TPU:0, one launch (start us, length us, event | category | flops | bytes accessed | tf_op | source)
XLA Modules:
  0.0 281.8 jit_solution(644162336561355162)
XLA Ops:
  7.3 3.1 %slice_bitcast_fusion = bf16[8,128,1024]{2,1,0:T(8,128)(2,1)} fusion(bf16[1,16,128,1024]{3,2,1,0:T(8,128)(2,1)} %param.9), kind=kLoop, calls=%fused_computation.3 | loop fusion | bytes 4194304 | tf_op jit(solution)/shard_map/slice | solution.py:276
  10.3 6.3 %all-to-all-start = ((bf16[8,128,1024]{2,1,0:T(8,128)(2,1)}), bf16[8,128,1024]{2,1,0:T(8,128)(2,1)S(1)}, u32[]{:S(2)}, u32[]{:S(2)}) async-start(bf16[8,128,1024]{2,1,0:T(8,128)(2,1)} %slice_bitcast_fusion), calls=%async_computation | async-start | bytes 4194304 | tf_op jit(solution)/shard_map/all_to_all | solution.py:276
  16.7 5.1 %constant_dynamic-slice_fusion = (bf16[1,2,1,256,1024]{4,3,2,1,0:T(8,128)(2,1)}, bf16[1,2,1,256,1024]{4,3,2,1,0:T(8,128)(2,1)}, bf16[1,2,1,256,1024]{4,3,2,1,0:T...) fusion(bf16[2,2,4,256,1024]{4,3,2,1,0:T(8,128)(2,1)} %bitcast.3, ...), kind=kLoop, calls=%fused_computation.4 | loop fusion | bytes 12582924 | tf_op jit(solution)/shard_map/dynamic_slice | solution.py:238
  21.8 2.4 pad_maximum_fusion
  25.6 1.5 collective-permute-start.1
  29.1 1.5 collective-permute-start.4
  31.2 27.6 %collective-permute-done.refs_9_.refs_12_ = bf16[704,1024]{1,0:T(8,128)(2,1)S(1)} collective-permute-done((bf16[704,1024]{1,0:T(8,128)(2,1)}, bf16[704,1024]{1,0:T(8,128)(2,1)S(1)}, u32[]{:S(2)}, u32[]{:S(2)}) %collective-permute-start) | collective-permute-done | bytes 1441824 | tf_op jit(solution)/shard_map/ppermute | solution.py:230
  58.8 2.4 collective-permute-start.5
  61.2 3.2 %slice.11 = bf16[8,128,1024]{2,1,0:T(8,128)(2,1)} slice(bf16[16,128,1024]{2,1,0:T(8,128)(2,1)} %bitcast.43), slice={[8:16], [0:128], [0:1024]} | slice | bytes 4194304 | tf_op jit(solution)/shard_map/slice | solution.py:276
  64.3 26.7 %all-to-all-done = bf16[8,128,1024]{2,1,0:T(8,128)(2,1)S(1)} async-done(((bf16[8,128,1024]{2,1,0:T(8,128)(2,1)}), bf16[8,128,1024]{2,1,0:T(8,128)(2,1)S(1)}, u32[]{:S(2)}, u32[]{:S(2)}) %all-to-all-start) | async-done | bytes 2097184 | tf_op jit(solution)/shard_map/all_to_all | solution.py:276
  92.3 4.4 %all-to-all-start.1 = ((bf16[8,128,1024]{2,1,0:T(8,128)(2,1)}), bf16[8,128,1024]{2,1,0:T(8,128)(2,1)}, u32[]{:S(2)}, u32[]{:S(2)}) async-start(bf16[8,128,1024]{2,1,0:T(8,128)(2,1)} %slice.11), calls=%async_computation.1 | async-start | bytes 4194304 | tf_op jit(solution)/shard_map/all_to_all | solution.py:276
  97.0 25.4 %factor_tiles.2 = (bf16[2,192,1024]{2,1,0:T(8,128)(2,1)}, bf16[2,2,192,1024]{3,2,1,0:T(8,128)(2,1)}) custom-call(s32[2]{0:T(128)} %pad_add_fusion.refs_0_, s32[16]{0:T(128)} %bitcast.53, s32[16]{0:T(128)} %bitcast.55, s32[16]{0:T(128)} %bitcast.57, s32[16]{0:T(128)} %bitcast.59, bf16[1024,1024]{1,0:T(8,128)(2,1)} %bitcast.44, ...), custom_call_target="tpu_custom_call" | custom-call | flops 3499999887360 | bytes 12582912 | tf_op jit(solution)/shard_map/factor_tiles/pallas_call | solution.py:137
  122.4 1.6 collective-permute-start.6
  126.1 9.3 %collective-permute-done.4.refs_13_ = bf16[512,1024]{1,0:T(8,128)(2,1)} collective-permute-done((bf16[512,1024]{1,0:T(8,128)(2,1)}, bf16[512,1024]{1,0:T(8,128)(2,1)}, u32[]{:S(2)}, u32[]{:S(2)}) %collective-permute-start.4) | collective-permute-done | bytes 1048608 | tf_op jit(solution)/shard_map/ppermute | solution.py:230
  135.7 36.0 %all-to-all-done.1 = bf16[8,128,1024]{2,1,0:T(8,128)(2,1)} async-done(((bf16[8,128,1024]{2,1,0:T(8,128)(2,1)}), bf16[8,128,1024]{2,1,0:T(8,128)(2,1)}, u32[]{:S(2)}, u32[]{:S(2)}) %all-to-all-start.1) | async-done | bytes 2097184 | tf_op jit(solution)/shard_map/all_to_all | solution.py:276
  171.7 25.1 %factor_tiles.3 = (bf16[2,192,1024]{2,1,0:T(8,128)(2,1)}, bf16[2,192,1024]{2,1,0:T(8,128)(2,1)}, bf16[2,192,1024]{2,1,0:T(8,128)(2,1)}) custom-call(s32[2]{0:T(128)} %pad_add_fusion.refs_0_, s32[16]{0:T(128)} %bitcast.54, s32[16]{0:T(128)} %bitcast.56, s32[16]{0:T(128)} %bitcast.58, s32[16]{0:T(128)} %bitcast.60, bf16[1024,1024]{1,0:T(8,128)(2,1)} %bitcast.19.refs_5_, ...), custom_call_target="tpu_custom_call" | custom-call | flops 3499999887360 | bytes 12582912 | tf_op jit(solution)/shard_map/factor_tiles/pallas_call | solution.py:137
  196.8 1.6 collective-permute-start.9
  198.4 1.6 collective-permute-start.13
  200.0 18.7 %collective-permute-done.9.refs_4_ = bf16[2,192,1024]{2,1,0:T(8,128)(2,1)} collective-permute-done((bf16[2,192,1024]{2,1,0:T(8,128)(2,1)}, bf16[2,192,1024]{2,1,0:T(8,128)(2,1)}, u32[]{:S(2)}, u32[]{:S(2)}) %collective-permute-start.9) | collective-permute-done | bytes 786464 | tf_op jit(solution)/shard_map/ppermute | solution.py:230
  223.4 11.3 %update_tile.2.refs_1_ = f32[1024,1024]{1,0:T(8,128)} custom-call(s32[2]{0:T(128)S(1)} %copy-done.3, bf16[1024,1024]{1,0:T(8,128)(2,1)} %refs_1_.1, bf16[8,2,192,1024]{3,2,1,0:T(8,128)(2,1)} %bitcast.49, bf16[2,2,192,1024]{3,2,1,0:T(8,128)(2,1)S(1)} %copy-done, bf16[2,2,192,1024]{3,2,1,0:T(8,128)(2,1)} %collective-permute-done.6.refs_4_, ...), custom_call_target="tpu_custom_call" | custom-call | flops 1500000026624 | bytes 20971520 | tf_op jit(solution)/shard_map/update_tile/pallas_call | solution.py:210
  234.7 4.8 %collective-permute-done.10.refs_5_ = bf16[2,192,1024]{2,1,0:T(8,128)(2,1)} collective-permute-done((bf16[2,192,1024]{2,1,0:T(8,128)(2,1)}, bf16[2,192,1024]{2,1,0:T(8,128)(2,1)}, u32[]{:S(2)}, u32[]{:S(2)}) %collective-permute-start.10) | collective-permute-done | bytes 786464 | tf_op jit(solution)/shard_map/ppermute | solution.py:230
  241.0 14.1 %collective-permute-done.11.refs_6_ = bf16[2,192,1024]{2,1,0:T(8,128)(2,1)} collective-permute-done((bf16[2,192,1024]{2,1,0:T(8,128)(2,1)}, bf16[2,192,1024]{2,1,0:T(8,128)(2,1)}, u32[]{:S(2)}, u32[]{:S(2)}) %collective-permute-start.11) | collective-permute-done | bytes 786464 | tf_op jit(solution)/shard_map/ppermute | solution.py:230
  256.5 7.0 %all-gather.11.cloned.1.call-done = bf16[16,192,1024]{2,1,0:T(8,128)(2,1)} async-done(((bf16[2,192,1024]{2,1,0:T(8,128)(2,1)}), bf16[16,192,1024]{2,1,0:T(8,128)(2,1)}) %all-gather.11.cloned.1.call-update) | async-done | bytes 6291472 | tf_op jit(solution)/shard_map/all_gather | solution.py:291
  263.5 11.6 %update_tile.3 = f32[1024,1024]{1,0:T(8,128)} custom-call(s32[2]{0:T(128)S(1)} %copy-done.3, f32[1024,1024]{1,0:T(8,128)} %update_tile.2.refs_1_, bf16[8,2,192,1024]{3,2,1,0:T(8,128)(2,1)} %bitcast.50, bf16[2,192,1024]{2,1,0:T(8,128)(2,1)S(1)} %copy-done.1, bf16[2,192,1024]{2,1,0:T(8,128)(2,1)} %collective-permute-done.9.refs_4_, ...), custom_call_target="tpu_custom_call" | custom-call | flops 1500000026624 | bytes 20971520 | tf_op jit(solution)/shard_map/update_tile/pallas_call | solution.py:210
  (42 shorter events, 16.2 us)
Async XLA Ops:
  6.5 90.4 %all-gather.7.cloned.1.call-start = ((), (), s32[]{:S(2)}) async-start(), calls=%async_computation.2 | async-start | bytes 3538944 | tf_op jit(solution)/shard_map/all_gather | solution.py:271
  10.3 80.7 %all-to-all-start = ((bf16[8,128,1024]{2,1,0:T(8,128)(2,1)}), bf16[8,128,1024]{2,1,0:T(8,128)(2,1)S(1)}, u32[]{:S(2)}, u32[]{:S(2)}) async-start(bf16[8,128,1024]{2,1,0:T(8,128)(2,1)} %slice_bitcast_fusion), calls=%async_computation | async-start | bytes 4194304 | tf_op jit(solution)/shard_map/all_to_all | solution.py:276
  24.2 34.6 %collective-permute-start = (bf16[704,1024]{1,0:T(8,128)(2,1)}, bf16[704,1024]{1,0:T(8,128)(2,1)S(1)}, u32[]{:S(2)}, u32[]{:S(2)}) collective-permute-start(bf16[704,1024]{1,0:T(8,128)(2,1)} %get-tuple-element.31), channel_id=1, source_target_pairs={{0,8},{8,0},{16,24},{24,16},{1,9},{9,1},{17,25},{25,17},{2,10},{10... | collective-permute-start | bytes 4325384 | tf_op jit(solution)/shard_map/ppermute | solution.py:230
  25.6 71.3 %collective-permute-start.1 = (bf16[704,1024]{1,0:T(8,128)(2,1)}, bf16[704,1024]{1,0:T(8,128)(2,1)}, u32[]{:S(2)}, u32[]{:S(2)}) collective-permute-start(bf16[704,1024]{1,0:T(8,128)(2,1)} %get-tuple-element.30), channel_id=1, source_target_pairs={{0,16},{8,24},{16,0},{24,8},{1,17},{9,25},{17,1},{25,9},{2,18},{10... | collective-permute-start | bytes 4325384 | tf_op jit(solution)/shard_map/ppermute | solution.py:230
  27.1 69.8 %collective-permute-start.2 = (bf16[704,1024]{1,0:T(8,128)(2,1)}, bf16[704,1024]{1,0:T(8,128)(2,1)}, u32[]{:S(2)}, u32[]{:S(2)}) collective-permute-start(bf16[704,1024]{1,0:T(8,128)(2,1)} %get-tuple-element.29), channel_id=1, source_target_pairs={{0,24},{8,16},{16,8},{24,0},{1,25},{9,17},{17,9},{25,1},{2,26},{10... | collective-permute-start | bytes 4325384 | tf_op jit(solution)/shard_map/ppermute | solution.py:230
  27.7 97.9 %collective-permute-start.3 = (bf16[512,1024]{1,0:T(8,128)(2,1)}, bf16[512,1024]{1,0:T(8,128)(2,1)}, u32[]{:S(2)}, u32[]{:S(2)}) collective-permute-start(bf16[512,1024]{1,0:T(8,128)(2,1)} %bitcast.20), channel_id=1, source_target_pairs={{0,8},{8,0},{16,24},{24,16},{1,9},{9,1},{17,25},{25,17},{2,10},{10... | collective-permute-start | bytes 3145736 | tf_op jit(solution)/shard_map/ppermute | solution.py:230
  29.1 106.3 %collective-permute-start.4 = (bf16[512,1024]{1,0:T(8,128)(2,1)}, bf16[512,1024]{1,0:T(8,128)(2,1)}, u32[]{:S(2)}, u32[]{:S(2)}) collective-permute-start(bf16[512,1024]{1,0:T(8,128)(2,1)} %bitcast.21), channel_id=1, source_target_pairs={{0,16},{8,24},{16,0},{24,8},{1,17},{9,25},{17,1},{25,9},{2,18},{10... | collective-permute-start | bytes 3145736 | tf_op jit(solution)/shard_map/ppermute | solution.py:230
  58.8 76.9 %collective-permute-start.5 = (bf16[512,1024]{1,0:T(8,128)(2,1)}, bf16[512,1024]{1,0:T(8,128)(2,1)}, u32[]{:S(2)}, u32[]{:S(2)}) collective-permute-start(bf16[512,1024]{1,0:T(8,128)(2,1)} %bitcast.22), channel_id=1, source_target_pairs={{0,24},{8,16},{16,8},{24,0},{1,25},{9,17},{17,9},{25,1},{2,26},{10... | collective-permute-start | bytes 3145736 | tf_op jit(solution)/shard_map/ppermute | solution.py:230
  92.3 79.4 %all-to-all-start.1 = ((bf16[8,128,1024]{2,1,0:T(8,128)(2,1)}), bf16[8,128,1024]{2,1,0:T(8,128)(2,1)}, u32[]{:S(2)}, u32[]{:S(2)}) async-start(bf16[8,128,1024]{2,1,0:T(8,128)(2,1)} %slice.11), calls=%async_computation.1 | async-start | bytes 4194304 | tf_op jit(solution)/shard_map/all_to_all | solution.py:276
  96.7 103.3 %all-gather.9.cloned.1.call-start = ((), (), s32[]{:S(2)}) async-start(), calls=%async_computation.3 | async-start | bytes 7077888 | tf_op jit(solution)/shard_map/all_gather | solution.py:291
  122.4 99.3 %collective-permute-start.6 = (bf16[2,2,192,1024]{3,2,1,0:T(8,128)(2,1)}, bf16[2,2,192,1024]{3,2,1,0:T(8,128)(2,1)}, u32[]{:S(2)}, u32[]{:S(2)}) collective-permute-start(bf16[2,2,192,1024]{3,2,1,0:T(8,128)(2,1)} %get-tuple-element.19.refs_3_), channel_id=1, source_target_pairs={{0,8},{8,0},{16,24},{24,16},{1,9},{9,1},{17,25},{25,17},{2,10},{10... | collective-permute-start | bytes 4718600 | tf_op jit(solution)/shard_map/ppermute | solution.py:230
  124.0 98.3 %collective-permute-start.7 = (bf16[2,2,192,1024]{3,2,1,0:T(8,128)(2,1)}, bf16[2,2,192,1024]{3,2,1,0:T(8,128)(2,1)}, u32[]{:S(2)}, u32[]{:S(2)}) collective-permute-start(bf16[2,2,192,1024]{3,2,1,0:T(8,128)(2,1)} %get-tuple-element.19.refs_3_), channel_id=1, source_target_pairs={{0,16},{8,24},{16,0},{24,8},{1,17},{9,25},{17,1},{25,9},{2,18},{10... | collective-permute-start | bytes 4718600 | tf_op jit(solution)/shard_map/ppermute | solution.py:230
  125.5 138.0 %all-gather.11.cloned.1.call-start = ((), (), s32[]{:S(2)}) async-start(), calls=%async_computation.4 | async-start | bytes 7077888 | tf_op jit(solution)/shard_map/all_gather | solution.py:291
  125.6 97.8 %collective-permute-start.8 = (bf16[2,2,192,1024]{3,2,1,0:T(8,128)(2,1)}, bf16[2,2,192,1024]{3,2,1,0:T(8,128)(2,1)}, u32[]{:S(2)}, u32[]{:S(2)}) collective-permute-start(bf16[2,2,192,1024]{3,2,1,0:T(8,128)(2,1)} %get-tuple-element.19.refs_3_), channel_id=1, source_target_pairs={{0,24},{8,16},{16,8},{24,0},{1,25},{9,17},{17,9},{25,1},{2,26},{10... | collective-permute-start | bytes 4718600 | tf_op jit(solution)/shard_map/ppermute | solution.py:230
  171.7 51.6 %copy-start = (bf16[2,2,192,1024]{3,2,1,0:T(8,128)(2,1)S(1)}, bf16[2,2,192,1024]{3,2,1,0:T(8,128)(2,1)}, u32[]{:S(2)}) copy-start(bf16[2,2,192,1024]{3,2,1,0:T(8,128)(2,1)} %get-tuple-element.19.refs_3_) | copy-start | bytes 4718596
  171.7 51.6 %copy-start.3 = (s32[2]{0:T(128)S(1)}, s32[2]{0:T(128)}, u32[]{:S(2)}) copy-start(s32[2]{0:T(128)} %pad_add_fusion.refs_0_) | copy-start | bytes 28
  196.8 21.9 %collective-permute-start.9 = (bf16[2,192,1024]{2,1,0:T(8,128)(2,1)}, bf16[2,192,1024]{2,1,0:T(8,128)(2,1)}, u32[]{:S(2)}, u32[]{:S(2)}) collective-permute-start(bf16[2,192,1024]{2,1,0:T(8,128)(2,1)} %get-tuple-element.21.refs_3_), channel_id=1, source_target_pairs={{0,8},{8,0},{16,24},{24,16},{1,9},{9,1},{17,25},{25,17},{2,10},{10... | collective-permute-start | bytes 2359304 | tf_op jit(solution)/shard_map/ppermute | solution.py:230
  198.4 21.8 %collective-permute-start.13 = (bf16[2,192,1024]{2,1,0:T(8,128)(2,1)}, bf16[2,192,1024]{2,1,0:T(8,128)(2,1)}, u32[]{:S(2)}, u32[]{:S(2)}) collective-permute-start(bf16[2,192,1024]{2,1,0:T(8,128)(2,1)} %get-tuple-element.22.refs_7_), channel_id=1, source_target_pairs={{0,16},{8,24},{16,0},{24,8},{1,17},{9,25},{17,1},{25,9},{2,18},{10... | collective-permute-start | bytes 2359304 | tf_op jit(solution)/shard_map/ppermute | solution.py:230
  218.7 20.8 %collective-permute-start.10 = (bf16[2,192,1024]{2,1,0:T(8,128)(2,1)}, bf16[2,192,1024]{2,1,0:T(8,128)(2,1)}, u32[]{:S(2)}, u32[]{:S(2)}) collective-permute-start(bf16[2,192,1024]{2,1,0:T(8,128)(2,1)} %get-tuple-element.21.refs_3_), channel_id=1, source_target_pairs={{0,16},{8,24},{16,0},{24,8},{1,17},{9,25},{17,1},{25,9},{2,18},{10... | collective-permute-start | bytes 2359304 | tf_op jit(solution)/shard_map/ppermute | solution.py:230
  220.2 20.8 %collective-permute-start.12 = (bf16[2,192,1024]{2,1,0:T(8,128)(2,1)}, bf16[2,192,1024]{2,1,0:T(8,128)(2,1)}, u32[]{:S(2)}, u32[]{:S(2)}) collective-permute-start(bf16[2,192,1024]{2,1,0:T(8,128)(2,1)} %get-tuple-element.22.refs_7_), channel_id=1, source_target_pairs={{0,8},{8,0},{16,24},{24,16},{1,9},{9,1},{17,25},{25,17},{2,10},{10... | collective-permute-start | bytes 2359304 | tf_op jit(solution)/shard_map/ppermute | solution.py:230
  221.7 33.3 %collective-permute-start.11 = (bf16[2,192,1024]{2,1,0:T(8,128)(2,1)}, bf16[2,192,1024]{2,1,0:T(8,128)(2,1)}, u32[]{:S(2)}, u32[]{:S(2)}) collective-permute-start(bf16[2,192,1024]{2,1,0:T(8,128)(2,1)} %collective-permute-done.9.refs_4_), channel_id=1, source_target_pairs={{0,16},{8,24},{16,0},{24,8},{1,17},{9,25},{17,1},{25,9},{2,18},{10... | collective-permute-start | bytes 2359304 | tf_op jit(solution)/shard_map/ppermute | solution.py:230
  222.2 34.2 %collective-permute-start.14 = (bf16[2,192,1024]{2,1,0:T(8,128)(2,1)}, bf16[2,192,1024]{2,1,0:T(8,128)(2,1)}, u32[]{:S(2)}, u32[]{:S(2)}) collective-permute-start(bf16[2,192,1024]{2,1,0:T(8,128)(2,1)} %collective-permute-done.13.refs_9_), channel_id=1, source_target_pairs={{0,8},{8,0},{16,24},{24,16},{1,9},{9,1},{17,25},{25,17},{2,10},{10... | collective-permute-start | bytes 2359304 | tf_op jit(solution)/shard_map/ppermute | solution.py:230
  223.4 40.1 %copy-start.1 = (bf16[2,192,1024]{2,1,0:T(8,128)(2,1)S(1)}, bf16[2,192,1024]{2,1,0:T(8,128)(2,1)}, u32[]{:S(2)}) copy-start(bf16[2,192,1024]{2,1,0:T(8,128)(2,1)} %get-tuple-element.21.refs_3_) | copy-start | bytes 2359300
  223.4 40.1 %copy-start.2 = (bf16[2,192,1024]{2,1,0:T(8,128)(2,1)S(1)}, bf16[2,192,1024]{2,1,0:T(8,128)(2,1)}, u32[]{:S(2)}) copy-start(bf16[2,192,1024]{2,1,0:T(8,128)(2,1)} %get-tuple-element.22.refs_7_) | copy-start | bytes 2359300
  (3 other events, 12.0 us)
Sparse Core Ops, SparseCore 0:
  9.0 75.1 all-gather.6
  125.6 72.5 all-gather.8
  200.1 63.3 all-gather.10

commit v2 on v1

--- a/solution.py
+++ b/solution.py
@@ -7,9 +7,9 @@
 from jax.experimental.pallas import tpu as pltpu
 from jax.sharding import PartitionSpec as P
 
-NB = 32
+NB = 64
 PANEL = 8
-VMEM_UPDATE = 50
+VMEM_UPDATE = 56
 HIGH = lax.Precision.HIGHEST
 NN = (((1,), (0,)), ((), ()))
 NT = (((1,), (1,)), ((), ()))
@@ -155,8 +155,8 @@
 
 def update_kernel(n_col, n_row, *refs):
     place, start, full_l = refs[:3]
-    out, ql, wl, left, acc, sem_l, sem_o = refs[-7:]
-    parts = refs[3:-7]
+    out, ql, wl, qwu, left, acc, tr, sem_l, sem_u, sem_t, sem_o = refs[-11:]
+    parts = refs[3:-11]
     if len(parts) == n_row:
         parts = [p.at[t] for t in range(n_col // n_row) for p in parts]
     my_row = place[0]
@@ -172,18 +172,34 @@
             pltpu.make_async_copy(full_l.at[at, 0], ql.at[at], sem_l.at[g, 0]),
         )
 
+    def load_u(i):
+        return pltpu.make_async_copy(parts[i], qwu.at[i], sem_u.at[i])
+
+    def load(g):
+        load_w, load_q = load_l(g)
+        load_w.start()
+        for i in range(g * n_row, (g + 1) * n_row):
+            load_u(i).start()
+        load_q.start()
+
+    load_start = pltpu.make_async_copy(start, tr, sem_t)
+    load(0)
     for g in range(rounds):
-        for c in load_l(g):
-            c.start()
-    for g in range(rounds):
-        mine = parts[g * n_row : (g + 1) * n_row]
+        mine = [qwu.at[i] for i in range(g * n_row, (g + 1) * n_row)]
         load_w, load_q = load_l(g)
         load_w.wait()
         mids = []
         for o, part in enumerate(mine):
+            load_u(g * n_row + o).wait()
             k = g * n_row + jnp.bitwise_xor(my_row, o)
             mids.append(mm(part[0], wl[k], NT).astype(jnp.bfloat16))
         load_q.wait()
+        if g + 1 < rounds:
+            load(g + 1)
+        if g == 0:
+            load_start.start()
+        if g == rounds - 1:
+            load_start.wait()
         for o, mid in enumerate(mids):
             k = g * n_row + jnp.bitwise_xor(my_row, o)
             left[o * width : (o + 1) * width, :] = mm(mid, ql[k], NN).astype(jnp.bfloat16)
@@ -194,7 +210,7 @@
             if g:
                 done = acc[at, :] + done
             if g == rounds - 1:
-                acc[at, :] = start[at, :].astype(jnp.float32) - done
+                acc[at, :] = tr[at, :].astype(jnp.float32) - done
                 pltpu.make_async_copy(acc.at[at], out.at[at], sem_o.at[b]).start()
             else:
                 acc[at, :] = done
@@ -210,14 +226,18 @@
     return pl.pallas_call(
         functools.partial(update_kernel, n_col, n_row),
         out_shape=jax.ShapeDtypeStruct(start.shape, jnp.float32),
-        in_specs=[SMEM, VMEM, HBM] + [VMEM] * len(parts),
+        in_specs=[SMEM, HBM, HBM] + [HBM] * len(parts),
         out_specs=HBM,
         scratch_shapes=[
             held,
             held,
+            pltpu.VMEM((n_col, 2, width, order), jnp.bfloat16),
             pltpu.VMEM((n_row * width, order), jnp.bfloat16),
             pltpu.VMEM(start.shape, jnp.float32),
+            pltpu.VMEM(start.shape, start.dtype),
             pltpu.SemaphoreType.DMA((n_col // n_row, 2)),
+            pltpu.SemaphoreType.DMA((n_col,)),
+            pltpu.SemaphoreType.DMA,
             pltpu.SemaphoreType.DMA((start.shape[0] // 256,)),
         ],
         compiler_params=pltpu.CompilerParams(vmem_limit_bytes=VMEM_UPDATE * 2**20),

time: 285 us -> 284 us (level)
  Pallas kernels: 73.3 us -> 67.3 us
  waiting for transfers between devices: 148 us -> 154 us
    pallas_call x2, Pallas kernels: 50.5 us -> 44.7 us  [factor(): pl.pallas_call(functools.partial(factor_kernel, n_col, n_row, chunk, join...]
    all_to_all x2, waiting for transfers between devices: 62.7 us -> 66.7 us  [local(): lax.all_to_all(mine_l[c * n_col:(c + 1) * n_col], 'col', 0, 0, tiled=True)]
  transfers between devices with their start and end apart: 20 -> 20, of which waited for: 11 -> 11; matrix products, arithmetic and copies ran while one was open for 5% -> 5% of each run, Pallas kernels for 22% -> 20%
where the time goes in v2:
time: 284 us; the launch traced here: 282 us
  waiting for transfers between devices  154 us (54%)
  Pallas kernels  67.3 us (24%)
  starting transfers between devices  31.1 us (11%)
  between operations  13.4 us (5%)
  local copies, waits for them, and re-layouts  12.8 us (5%)
  other arithmetic  2.9 us (1%)
    ppermute x15, waiting for transfers between devices, shift(): return lax.ppermute(x, axis, [(i, move(i)) for i in range(size)])  79.6 us
    all_to_all x2, waiting for transfers between devices, local(): lax.all_to_all(mine_l[c * n_col:(c + 1) * n_col], 'col', 0, 0, tiled=True)  66.7 us
    pallas_call x2, Pallas kernels, factor(): pl.pallas_call(functools.partial(factor_kernel, n_col, n_row, chunk, join...  44.7 us
    pallas_call x2, Pallas kernels, update(): pl.pallas_call(functools.partial(update_kernel, n_col, n_row), out_shape=...  22.6 us
    ppermute x15, starting transfers between devices, shift(): return lax.ppermute(x, axis, [(i, move(i)) for i in range(size)])  20.1 us
    all_to_all x2, starting transfers between devices, local(): lax.all_to_all(mine_l[c * n_col:(c + 1) * n_col], 'col', 0, 0, tiled=True)  10.7 us
    all_gather x2, waiting for transfers between devices, local(): full_l = lax.all_gather(made_l[None], 'col', axis=0, tiled=True)  7.08 us
    slice x2, local copies, waits for them, and re-layouts, local(): mine_l[c * n_col:(c + 1) * n_col]  6.28 us
  transfers between devices with their start and end apart: 20, of which 11 were waited for; matrix products, arithmetic and copies ran while one was open for 5% of the time, Pallas kernels for 20%

profile of v2, /device:TPU:0, one launch (start us, length us, event | category | flops | bytes accessed | tf_op | source)
XLA Modules:
  0.0 281.6 jit_solution(2368351890750116108)
XLA Ops:
  7.3 3.1 %slice_bitcast_fusion = bf16[8,128,1024]{2,1,0:T(8,128)(2,1)} fusion(bf16[1,16,128,1024]{3,2,1,0:T(8,128)(2,1)} %param.9), kind=kLoop, calls=%fused_computation.3 | loop fusion | bytes 4194304 | tf_op jit(solution)/shard_map/slice | solution.py:296
  10.3 6.3 %all-to-all-start = ((bf16[8,128,1024]{2,1,0:T(8,128)(2,1)}), bf16[8,128,1024]{2,1,0:T(8,128)(2,1)S(1)}, u32[]{:S(2)}, u32[]{:S(2)}) async-start(bf16[8,128,1024]{2,1,0:T(8,128)(2,1)} %slice_bitcast_fusion), calls=%async_computation | async-start | bytes 4194304 | tf_op jit(solution)/shard_map/all_to_all | solution.py:296
  16.7 5.1 %constant_dynamic-slice_fusion = (bf16[1,2,1,256,1024]{4,3,2,1,0:T(8,128)(2,1)}, bf16[1,2,1,256,1024]{4,3,2,1,0:T(8,128)(2,1)}, bf16[1,2,1,256,1024]{4,3,2,1,0:T...) fusion(bf16[2,2,4,256,1024]{4,3,2,1,0:T(8,128)(2,1)} %bitcast.3, ...), kind=kLoop, calls=%fused_computation.4 | loop fusion | bytes 12582924 | tf_op jit(solution)/shard_map/dynamic_slice | solution.py:258
  21.8 2.3 pad_maximum_fusion
  25.5 1.5 collective-permute-start.1
  29.0 1.5 collective-permute-start.4
  31.2 27.5 %collective-permute-done.refs_9_.refs_12_ = bf16[704,1024]{1,0:T(8,128)(2,1)S(1)} collective-permute-done((bf16[704,1024]{1,0:T(8,128)(2,1)}, bf16[704,1024]{1,0:T(8,128)(2,1)S(1)}, u32[]{:S(2)}, u32[]{:S(2)}) %collective-permute-start) | collective-permute-done | bytes 1441824 | tf_op jit(solution)/shard_map/ppermute | solution.py:250
  58.7 2.4 collective-permute-start.5
  61.1 3.2 %slice.11 = bf16[8,128,1024]{2,1,0:T(8,128)(2,1)} slice(bf16[16,128,1024]{2,1,0:T(8,128)(2,1)} %bitcast.43), slice={[8:16], [0:128], [0:1024]} | slice | bytes 4194304 | tf_op jit(solution)/shard_map/slice | solution.py:296
  64.3 26.7 %all-to-all-done = bf16[8,128,1024]{2,1,0:T(8,128)(2,1)S(1)} async-done(((bf16[8,128,1024]{2,1,0:T(8,128)(2,1)}), bf16[8,128,1024]{2,1,0:T(8,128)(2,1)S(1)}, u32[]{:S(2)}, u32[]{:S(2)}) %all-to-all-start) | async-done | bytes 2097184 | tf_op jit(solution)/shard_map/all_to_all | solution.py:296
  92.3 4.4 %all-to-all-start.1 = ((bf16[8,128,1024]{2,1,0:T(8,128)(2,1)}), bf16[8,128,1024]{2,1,0:T(8,128)(2,1)}, u32[]{:S(2)}, u32[]{:S(2)}) async-start(bf16[8,128,1024]{2,1,0:T(8,128)(2,1)} %slice.11), calls=%async_computation.1 | async-start | bytes 4194304 | tf_op jit(solution)/shard_map/all_to_all | solution.py:296
  97.0 22.6 %factor_tiles.2 = (bf16[2,192,1024]{2,1,0:T(8,128)(2,1)}, bf16[2,2,192,1024]{3,2,1,0:T(8,128)(2,1)}) custom-call(s32[2]{0:T(128)} %pad_add_fusion.refs_0_, s32[16]{0:T(128)} %bitcast.53, s32[16]{0:T(128)} %bitcast.55, s32[16]{0:T(128)} %bitcast.57, s32[16]{0:T(128)} %bitcast.59, bf16[1024,1024]{1,0:T(8,128)(2,1)} %bitcast.44, ...), custom_call_target="tpu_custom_call" | custom-call | flops 3499999887360 | bytes 12582912 | tf_op jit(solution)/shard_map/factor_tiles/pallas_call | solution.py:137
  119.5 1.6 collective-permute-start.6
  123.2 12.1 %collective-permute-done.4.refs_13_ = bf16[512,1024]{1,0:T(8,128)(2,1)} collective-permute-done((bf16[512,1024]{1,0:T(8,128)(2,1)}, bf16[512,1024]{1,0:T(8,128)(2,1)}, u32[]{:S(2)}, u32[]{:S(2)}) %collective-permute-start.4) | collective-permute-done | bytes 1048608 | tf_op jit(solution)/shard_map/ppermute | solution.py:250
  135.6 39.9 %all-to-all-done.1 = bf16[8,128,1024]{2,1,0:T(8,128)(2,1)} async-done(((bf16[8,128,1024]{2,1,0:T(8,128)(2,1)}), bf16[8,128,1024]{2,1,0:T(8,128)(2,1)}, u32[]{:S(2)}, u32[]{:S(2)}) %all-to-all-start.1) | async-done | bytes 2097184 | tf_op jit(solution)/shard_map/all_to_all | solution.py:296
  175.5 22.1 %factor_tiles.3 = (bf16[2,192,1024]{2,1,0:T(8,128)(2,1)}, bf16[2,192,1024]{2,1,0:T(8,128)(2,1)}, bf16[2,192,1024]{2,1,0:T(8,128)(2,1)}) custom-call(s32[2]{0:T(128)} %pad_add_fusion.refs_0_, s32[16]{0:T(128)} %bitcast.54, s32[16]{0:T(128)} %bitcast.56, s32[16]{0:T(128)} %bitcast.58, s32[16]{0:T(128)} %bitcast.60, bf16[1024,1024]{1,0:T(8,128)(2,1)} %bitcast.19.refs_5_, ...), custom_call_target="tpu_custom_call" | custom-call | flops 3499999887360 | bytes 12582912 | tf_op jit(solution)/shard_map/factor_tiles/pallas_call | solution.py:137
  197.7 1.6 collective-permute-start.9
  200.8 17.9 %collective-permute-done.9.refs_4_ = bf16[2,192,1024]{2,1,0:T(8,128)(2,1)} collective-permute-done((bf16[2,192,1024]{2,1,0:T(8,128)(2,1)}, bf16[2,192,1024]{2,1,0:T(8,128)(2,1)}, u32[]{:S(2)}, u32[]{:S(2)}) %collective-permute-start.9) | collective-permute-done | bytes 786464 | tf_op jit(solution)/shard_map/ppermute | solution.py:250
  223.3 11.2 %update_tile.2.refs_1_ = f32[1024,1024]{1,0:T(8,128)} custom-call(s32[2]{0:T(128)} %pad_add_fusion.refs_0_, bf16[1024,1024]{1,0:T(8,128)(2,1)} %refs_1_.1, bf16[8,2,192,1024]{3,2,1,0:T(8,128)(2,1)} %bitcast.49, bf16[2,2,192,1024]{3,2,1,0:T(8,128)(2,1)} %get-tuple-element.19.refs_3_, bf16[2,2,192,1024]{3,2,1,0:T(8,128)(2,1)} %collective-permute-done.6.refs_4_, ...), custom_call_target="tpu_custom_call" | custom-call | flops 1500000026624 | bytes 20971520 | tf_op jit(solution)/shard_map/update_tile/pallas_call | solution.py:226
  234.4 5.0 %collective-permute-done.10.refs_5_ = bf16[2,192,1024]{2,1,0:T(8,128)(2,1)} collective-permute-done((bf16[2,192,1024]{2,1,0:T(8,128)(2,1)}, bf16[2,192,1024]{2,1,0:T(8,128)(2,1)}, u32[]{:S(2)}, u32[]{:S(2)}) %collective-permute-start.10) | collective-permute-done | bytes 786464 | tf_op jit(solution)/shard_map/ppermute | solution.py:250
  239.4 1.5 collective-permute-done.12.refs_8_
  241.0 14.1 %collective-permute-done.11.refs_6_ = bf16[2,192,1024]{2,1,0:T(8,128)(2,1)} collective-permute-done((bf16[2,192,1024]{2,1,0:T(8,128)(2,1)}, bf16[2,192,1024]{2,1,0:T(8,128)(2,1)}, u32[]{:S(2)}, u32[]{:S(2)}) %collective-permute-start.11) | collective-permute-done | bytes 786464 | tf_op jit(solution)/shard_map/ppermute | solution.py:250
  256.3 7.1 %all-gather.11.cloned.1.call-done = bf16[16,192,1024]{2,1,0:T(8,128)(2,1)} async-done(((bf16[2,192,1024]{2,1,0:T(8,128)(2,1)}), bf16[16,192,1024]{2,1,0:T(8,128)(2,1)}) %all-gather.11.cloned.1.call-update) | async-done | bytes 6291472 | tf_op jit(solution)/shard_map/all_gather | solution.py:311
  263.4 11.5 %update_tile.3 = f32[1024,1024]{1,0:T(8,128)} custom-call(s32[2]{0:T(128)} %pad_add_fusion.refs_0_, f32[1024,1024]{1,0:T(8,128)} %update_tile.2.refs_1_, bf16[8,2,192,1024]{3,2,1,0:T(8,128)(2,1)} %bitcast.50, bf16[2,192,1024]{2,1,0:T(8,128)(2,1)} %get-tuple-element.21.refs_3_, bf16[2,192,1024]{2,1,0:T(8,128)(2,1)} %collective-permute-done.9.refs_4_, ...), custom_call_target="tpu_custom_call" | custom-call | flops 1500000026624 | bytes 20971520 | tf_op jit(solution)/shard_map/update_tile/pallas_call | solution.py:226
  (34 shorter events, 16.1 us)
Async XLA Ops:
  6.5 90.4 %all-gather.7.cloned.1.call-start = ((), (), s32[]{:S(2)}) async-start(), calls=%async_computation.2 | async-start | bytes 3538944 | tf_op jit(solution)/shard_map/all_gather | solution.py:291
  10.3 80.7 %all-to-all-start = ((bf16[8,128,1024]{2,1,0:T(8,128)(2,1)}), bf16[8,128,1024]{2,1,0:T(8,128)(2,1)S(1)}, u32[]{:S(2)}, u32[]{:S(2)}) async-start(bf16[8,128,1024]{2,1,0:T(8,128)(2,1)} %slice_bitcast_fusion), calls=%async_computation | async-start | bytes 4194304 | tf_op jit(solution)/shard_map/all_to_all | solution.py:296
  16.7 5.2 %copy-start.1 = (bf16[1,1,1024,192]{2,3,1,0:T(8,128)(2,1)S(1)}, bf16[1,1,1024,192]{2,3,1,0:T(8,128)(2,1)}, u32[]{:S(2)}) copy-start(bf16[1,1,1024,192]{2,3,1,0:T(8,128)(2,1)} %param.11) | copy-start | bytes 1179652
  24.1 34.6 %collective-permute-start = (bf16[704,1024]{1,0:T(8,128)(2,1)}, bf16[704,1024]{1,0:T(8,128)(2,1)S(1)}, u32[]{:S(2)}, u32[]{:S(2)}) collective-permute-start(bf16[704,1024]{1,0:T(8,128)(2,1)} %get-tuple-element.31), channel_id=1, source_target_pairs={{0,8},{8,0},{16,24},{24,16},{1,9},{9,1},{17,25},{25,17},{2,10},{10... | collective-permute-start | bytes 4325384 | tf_op jit(solution)/shard_map/ppermute | solution.py:250
  25.5 71.4 %collective-permute-start.1 = (bf16[704,1024]{1,0:T(8,128)(2,1)}, bf16[704,1024]{1,0:T(8,128)(2,1)}, u32[]{:S(2)}, u32[]{:S(2)}) collective-permute-start(bf16[704,1024]{1,0:T(8,128)(2,1)} %get-tuple-element.30), channel_id=1, source_target_pairs={{0,16},{8,24},{16,0},{24,8},{1,17},{9,25},{17,1},{25,9},{2,18},{10... | collective-permute-start | bytes 4325384 | tf_op jit(solution)/shard_map/ppermute | solution.py:250
  27.1 69.9 %collective-permute-start.2 = (bf16[704,1024]{1,0:T(8,128)(2,1)}, bf16[704,1024]{1,0:T(8,128)(2,1)}, u32[]{:S(2)}, u32[]{:S(2)}) collective-permute-start(bf16[704,1024]{1,0:T(8,128)(2,1)} %get-tuple-element.29), channel_id=1, source_target_pairs={{0,24},{8,16},{16,8},{24,0},{1,25},{9,17},{17,9},{25,1},{2,26},{10... | collective-permute-start | bytes 4325384 | tf_op jit(solution)/shard_map/ppermute | solution.py:250
  27.6 95.1 %collective-permute-start.3 = (bf16[512,1024]{1,0:T(8,128)(2,1)}, bf16[512,1024]{1,0:T(8,128)(2,1)}, u32[]{:S(2)}, u32[]{:S(2)}) collective-permute-start(bf16[512,1024]{1,0:T(8,128)(2,1)} %bitcast.20), channel_id=1, source_target_pairs={{0,8},{8,0},{16,24},{24,16},{1,9},{9,1},{17,25},{25,17},{2,10},{10... | collective-permute-start | bytes 3145736 | tf_op jit(solution)/shard_map/ppermute | solution.py:250
  29.0 106.3 %collective-permute-start.4 = (bf16[512,1024]{1,0:T(8,128)(2,1)}, bf16[512,1024]{1,0:T(8,128)(2,1)}, u32[]{:S(2)}, u32[]{:S(2)}) collective-permute-start(bf16[512,1024]{1,0:T(8,128)(2,1)} %bitcast.21), channel_id=1, source_target_pairs={{0,16},{8,24},{16,0},{24,8},{1,17},{9,25},{17,1},{25,9},{2,18},{10... | collective-permute-start | bytes 3145736 | tf_op jit(solution)/shard_map/ppermute | solution.py:250
  58.7 5.6 %copy-start.2 = (bf16[704,1024]{1,0:T(8,128)(2,1)}, bf16[704,1024]{1,0:T(8,128)(2,1)S(1)}, u32[]{:S(2)}) copy-start(bf16[704,1024]{1,0:T(8,128)(2,1)S(1)} %collective-permute-done.refs_9_.refs_12_) | copy-start | bytes 4325380
  58.7 76.9 %collective-permute-start.5 = (bf16[512,1024]{1,0:T(8,128)(2,1)}, bf16[512,1024]{1,0:T(8,128)(2,1)}, u32[]{:S(2)}, u32[]{:S(2)}) collective-permute-start(bf16[512,1024]{1,0:T(8,128)(2,1)} %bitcast.22), channel_id=1, source_target_pairs={{0,24},{8,16},{16,8},{24,0},{1,25},{9,17},{17,9},{25,1},{2,26},{10... | collective-permute-start | bytes 3145736 | tf_op jit(solution)/shard_map/ppermute | solution.py:250
  91.0 1.3 copy-start
  92.3 83.2 %all-to-all-start.1 = ((bf16[8,128,1024]{2,1,0:T(8,128)(2,1)}), bf16[8,128,1024]{2,1,0:T(8,128)(2,1)}, u32[]{:S(2)}, u32[]{:S(2)}) async-start(bf16[8,128,1024]{2,1,0:T(8,128)(2,1)} %slice.11), calls=%async_computation.1 | async-start | bytes 4194304 | tf_op jit(solution)/shard_map/all_to_all | solution.py:296
  96.7 104.1 %all-gather.9.cloned.1.call-start = ((), (), s32[]{:S(2)}) async-start(), calls=%async_computation.3 | async-start | bytes 7077888 | tf_op jit(solution)/shard_map/all_gather | solution.py:311
  119.5 102.1 %collective-permute-start.6 = (bf16[2,2,192,1024]{3,2,1,0:T(8,128)(2,1)}, bf16[2,2,192,1024]{3,2,1,0:T(8,128)(2,1)}, u32[]{:S(2)}, u32[]{:S(2)}) collective-permute-start(bf16[2,2,192,1024]{3,2,1,0:T(8,128)(2,1)} %get-tuple-element.19.refs_3_), channel_id=1, source_target_pairs={{0,8},{8,0},{16,24},{24,16},{1,9},{9,1},{17,25},{25,17},{2,10},{10... | collective-permute-start | bytes 4718600 | tf_op jit(solution)/shard_map/ppermute | solution.py:250
  121.1 101.1 %collective-permute-start.7 = (bf16[2,2,192,1024]{3,2,1,0:T(8,128)(2,1)}, bf16[2,2,192,1024]{3,2,1,0:T(8,128)(2,1)}, u32[]{:S(2)}, u32[]{:S(2)}) collective-permute-start(bf16[2,2,192,1024]{3,2,1,0:T(8,128)(2,1)} %get-tuple-element.19.refs_3_), channel_id=1, source_target_pairs={{0,16},{8,24},{16,0},{24,8},{1,17},{9,25},{17,1},{25,9},{2,18},{10... | collective-permute-start | bytes 4718600 | tf_op jit(solution)/shard_map/ppermute | solution.py:250
  122.6 140.7 %all-gather.11.cloned.1.call-start = ((), (), s32[]{:S(2)}) async-start(), calls=%async_computation.4 | async-start | bytes 7077888 | tf_op jit(solution)/shard_map/all_gather | solution.py:311
  122.7 100.6 %collective-permute-start.8 = (bf16[2,2,192,1024]{3,2,1,0:T(8,128)(2,1)}, bf16[2,2,192,1024]{3,2,1,0:T(8,128)(2,1)}, u32[]{:S(2)}, u32[]{:S(2)}) collective-permute-start(bf16[2,2,192,1024]{3,2,1,0:T(8,128)(2,1)} %get-tuple-element.19.refs_3_), channel_id=1, source_target_pairs={{0,24},{8,16},{16,8},{24,0},{1,25},{9,17},{17,9},{25,1},{2,26},{10... | collective-permute-start | bytes 4718600 | tf_op jit(solution)/shard_map/ppermute | solution.py:250
  197.7 21.0 %collective-permute-start.9 = (bf16[2,192,1024]{2,1,0:T(8,128)(2,1)}, bf16[2,192,1024]{2,1,0:T(8,128)(2,1)}, u32[]{:S(2)}, u32[]{:S(2)}) collective-permute-start(bf16[2,192,1024]{2,1,0:T(8,128)(2,1)} %get-tuple-element.21.refs_3_), channel_id=1, source_target_pairs={{0,8},{8,0},{16,24},{24,16},{1,9},{9,1},{17,25},{25,17},{2,10},{10... | collective-permute-start | bytes 2359304 | tf_op jit(solution)/shard_map/ppermute | solution.py:250
  199.2 20.9 %collective-permute-start.13 = (bf16[2,192,1024]{2,1,0:T(8,128)(2,1)}, bf16[2,192,1024]{2,1,0:T(8,128)(2,1)}, u32[]{:S(2)}, u32[]{:S(2)}) collective-permute-start(bf16[2,192,1024]{2,1,0:T(8,128)(2,1)} %get-tuple-element.22.refs_7_), channel_id=1, source_target_pairs={{0,16},{8,24},{16,0},{24,8},{1,17},{9,25},{17,1},{25,9},{2,18},{10... | collective-permute-start | bytes 2359304 | tf_op jit(solution)/shard_map/ppermute | solution.py:250
  218.7 20.8 %collective-permute-start.10 = (bf16[2,192,1024]{2,1,0:T(8,128)(2,1)}, bf16[2,192,1024]{2,1,0:T(8,128)(2,1)}, u32[]{:S(2)}, u32[]{:S(2)}) collective-permute-start(bf16[2,192,1024]{2,1,0:T(8,128)(2,1)} %get-tuple-element.21.refs_3_), channel_id=1, source_target_pairs={{0,16},{8,24},{16,0},{24,8},{1,17},{9,25},{17,1},{25,9},{2,18},{10... | collective-permute-start | bytes 2359304 | tf_op jit(solution)/shard_map/ppermute | solution.py:250
  220.2 20.8 %collective-permute-start.12 = (bf16[2,192,1024]{2,1,0:T(8,128)(2,1)}, bf16[2,192,1024]{2,1,0:T(8,128)(2,1)}, u32[]{:S(2)}, u32[]{:S(2)}) collective-permute-start(bf16[2,192,1024]{2,1,0:T(8,128)(2,1)} %get-tuple-element.22.refs_7_), channel_id=1, source_target_pairs={{0,8},{8,0},{16,24},{24,16},{1,9},{9,1},{17,25},{25,17},{2,10},{10... | collective-permute-start | bytes 2359304 | tf_op jit(solution)/shard_map/ppermute | solution.py:250
  221.7 33.3 %collective-permute-start.11 = (bf16[2,192,1024]{2,1,0:T(8,128)(2,1)}, bf16[2,192,1024]{2,1,0:T(8,128)(2,1)}, u32[]{:S(2)}, u32[]{:S(2)}) collective-permute-start(bf16[2,192,1024]{2,1,0:T(8,128)(2,1)} %collective-permute-done.9.refs_4_), channel_id=1, source_target_pairs={{0,16},{8,24},{16,0},{24,8},{1,17},{9,25},{17,1},{25,9},{2,18},{10... | collective-permute-start | bytes 2359304 | tf_op jit(solution)/shard_map/ppermute | solution.py:250
  222.2 34.1 %collective-permute-start.14 = (bf16[2,192,1024]{2,1,0:T(8,128)(2,1)}, bf16[2,192,1024]{2,1,0:T(8,128)(2,1)}, u32[]{:S(2)}, u32[]{:S(2)}) collective-permute-start(bf16[2,192,1024]{2,1,0:T(8,128)(2,1)} %collective-permute-done.13.refs_9_), channel_id=1, source_target_pairs={{0,8},{8,0},{16,24},{24,16},{1,9},{9,1},{17,25},{25,17},{2,10},{10... | collective-permute-start | bytes 2359304 | tf_op jit(solution)/shard_map/ppermute | solution.py:250
Sparse Core Ops, SparseCore 0:
  9.0 75.1 all-gather.6
  122.8 75.2 all-gather.8
  200.9 62.3 all-gather.10
